TPU v7x, 128 devices: a whole 4x4x4 slice. The times are simulated.
128 devices in a mesh: expert: 8 (over z, core), shard: 16 (over y, x).
Axes of the slice: x: 4, y: 4, z: 4, core: 2. Of those that a mesh axis runs over, the one named last changes fastest.
Arguments:
- tokens: bfloat16 [16384, 896], P(('expert', 'shard')), may hold values from -6 to 6
- routes: int32 [16384, 2], P(('expert', 'shard')), may hold values from 0 to 7, all different within a row; in each aligned block of 128 rows (0 to 127, 128 to 255, ...) at most 48 rows name the same one
- gate_num: int32 [16384, 2], P(('expert', 'shard')), may hold values from 1 to 15
- student_gate: bfloat16 [8, 896, 4864], P('expert', None, 'shard'), may hold values from -0.1875 to 0.1875
- student_up: bfloat16 [8, 896, 4864], P('expert', None, 'shard'), may hold values from -0.1875 to 0.1875
- student_down: bfloat16 [8, 4864, 896], P('expert', 'shard'), may hold values from -0.078125 to 0.078125
- teacher_gate: bfloat16 [8, 896, 4864], P('expert', None, 'shard'), may hold values from -0.1875 to 0.1875
- teacher_up: bfloat16 [8, 896, 4864], P('expert', None, 'shard'), may hold values from -0.1875 to 0.1875
- teacher_down: bfloat16 [8, 4864, 896], P('expert', 'shard'), may hold values from -0.078125 to 0.078125
Outputs:
- residual: bfloat16 [16384, 896], P(('expert', 'shard'))
Inputs may be any that keep to these rules, and one draw needn't show every extreme that they name: `routes`: each row names two different experts. Among the rows of one device no expert is named by more than 48 rows, and in every draw some expert is named by exactly 48 rows of some device.
All inputs are finite; a program needn't handle non-finite values.
Results may differ from a plain program's by a relative error of at most 0.0049.
Values may be sent and summed in bfloat16 or wider, within the bound.
No kernel may reach another device: no remote copies, remote signals or barrier semaphores. Data moves between devices by JAX's collectives and lax.ppermute only.
A program may use at most 128 MiB of HBM per device.

v0:
```python
import functools

import jax
import jax.numpy as jnp
from jax import lax
from jax.experimental import pallas as pl
from jax.experimental.pallas import tpu as pltpu
from jax.sharding import PartitionSpec as P

AXES = ("expert", "shard")
BF16 = jnp.bfloat16
F32 = jnp.float32
CAP = 48
EXPERTS = 8
STEPS = (2, 1, 3, 0)
VMEM_LIMIT = 16 * 1024 * 1024


def dev(z, c, y, x):
    return ((z % 4 * 2 + c % 2) * 4 + y % 4) * 4 + x % 4


COORDS = [(z, c, y, x) for z in range(4) for c in range(2) for y in range(4) for x in range(4)]


def ring(step, weights):
    return [
        (dev(z, c, y, x), dev(z, c, y, x + step) if (c == 0) == weights else dev(z, c, y + step, x))
        for z, c, y, x in COORDS
    ]


def cross(step):
    return [(dev(z, c, y, x), dev(z, 1 - c, y + step, x) if c == 0 else dev(z, 1 - c, y, x + step)) for z, c, y, x in COORDS]


def along_z(step):
    return [(dev(z, c, y, x), dev(z + step, c, y, x)) for z, c, y, x in COORDS]


def send(value, pairs):
    return lax.ppermute(value, AXES, pairs)


def barrier(*values):
    return lax.optimization_barrier(values)


def whole(count, space=pltpu.VMEM):
    return [pl.BlockSpec(memory_space=space)] * count


def params(limit=VMEM_LIMIT):
    return pltpu.CompilerParams(vmem_limit_bytes=limit)


def near(value):
    return pltpu.with_memory_space_constraint(value, pltpu.VMEM)


def places(routes_ref):
    tokens = routes_ref.shape[1]
    first, second = routes_ref[0:1, :], routes_ref[1:2, :]
    expert = lax.broadcasted_iota(jnp.int32, (16, tokens), 0)
    named = ((expert == first).astype(F32) + (expert == second).astype(F32)).astype(BF16)
    before = lax.broadcasted_iota(jnp.int32, (tokens, tokens), 0) < lax.broadcasted_iota(jnp.int32, (tokens, tokens), 1)
    earlier = jnp.dot(named, before.astype(F32).astype(BF16), preferred_element_type=F32)
    found = []
    for ids, extra in ((first, 0), (second, (first == second).astype(jnp.int32))):
        slot = jnp.sum(jnp.where(expert == ids, earlier, 0.0), axis=0, keepdims=True).astype(jnp.int32) + extra
        found.append(ids * CAP + slot)
    return found


def pack_kernel(n_rest, *refs):
    weight_refs, rest, packed_ref = refs[:3], refs[3 : 3 + n_rest], refs[3 + n_rest]
    sems = refs[-1]
    units = weight_refs[0].shape[0]
    ins = [
        pltpu.make_async_copy(ref, packed_ref.at[pl.ds(i * units, units)], sems.at[i]) for i, ref in enumerate(weight_refs)
    ]
    for copy in ins:
        copy.start()
    if rest:
        routes_ref, tokens_ref = rest
        first, second = places(routes_ref)
        slots = lax.broadcasted_iota(jnp.int32, (EXPERTS * CAP, tokens_ref.shape[0]), 0)
        chosen = ((slots == first) | (slots == second)).astype(F32).astype(BF16)
        refs[4 + n_rest][...] = jnp.dot(chosen, tokens_ref[...], preferred_element_type=F32).astype(BF16)
    for copy in ins:
        copy.wait()


def pack(weights, *rest):
    gate, up, down = weights
    units, width = down.shape
    rows = [pltpu.VMEM((EXPERTS * CAP, width), BF16)] if rest else []
    return pl.pallas_call(
        functools.partial(pack_kernel, len(rest)),
        out_shape=[pltpu.VMEM((3 * units, width), BF16)] + rows,
        in_specs=whole(3, pltpu.HBM) + whole(len(rest)),
        out_specs=whole(1 + len(rows)),
        scratch_shapes=[pltpu.SemaphoreType.DMA((3,))],
        compiler_params=params(58 * 1024 * 1024 if rest else VMEM_LIMIT),
        cost_estimate=pl.CostEstimate(flops=100_000_000, bytes_accessed=4_000_000, transcendentals=0),
        name="pack_weights",
    )(gate.T, up.T, down, *rest)


def split_kernel(cut, *refs):
    n = len(refs) // 3
    for i in range(n):
        units = refs[i].shape[0] // 3
        for ref, first, count in ((refs[n + 2 * i], 0, cut), (refs[n + 2 * i + 1], cut, units - cut)):
            for k in range(3):
                ref[k * count : (k + 1) * count] = refs[i][k * units + first : k * units + first + count]


def split(cut, *packed):
    shapes = [pltpu.VMEM((3 * n, p.shape[1]), BF16) for p in packed for n in (cut, p.shape[0] // 3 - cut)]
    return pl.pallas_call(
        functools.partial(split_kernel, cut),
        out_shape=shapes,
        in_specs=whole(len(packed)),
        out_specs=whole(len(shapes)),
        compiler_params=params(),
        cost_estimate=pl.CostEstimate(flops=0, bytes_accessed=6_000_000, transcendentals=0),
        name="split_weights",
    )(*(near(p) for p in packed))


def shares_kernel(routes_ref, gates_ref, high_ref, low_ref):
    first, second = places(routes_ref)
    gates = gates_ref[...].astype(F32)
    share = gates / jnp.sum(gates, axis=0, keepdims=True)
    slots = lax.broadcasted_iota(jnp.int32, (EXPERTS * CAP, routes_ref.shape[1]), 0)
    weight = jnp.where(slots == first, share[0:1], 0.0) + jnp.where(slots == second, share[1:2], 0.0)
    weight = weight.T
    high = weight.astype(BF16)
    high_ref[...] = high
    low_ref[...] = (weight - high.astype(F32)).astype(BF16)


def shares(routes, gates):
    tokens = routes.shape[1]
    return pl.pallas_call(
        shares_kernel,
        out_shape=[jax.ShapeDtypeStruct((tokens, EXPERTS * CAP), BF16)] * 2,
        in_specs=whole(2),
        out_specs=whole(2),
        compiler_params=params(),
        cost_estimate=pl.CostEstimate(flops=10_000_000, bytes_accessed=1_000_000, transcendentals=0),
        name="gate_shares",
    )(routes, gates)


def block_of(place):
    return pl.ds(pl.multiple_of(place * CAP, CAP), CAP)


def halves_kernel(here_ref, own_ref, far_ref, keep_ref, give_ref):
    core = here_ref[0] & 1
    for z in range(EXPERTS // 2):
        to = slice(z * CAP, (z + 1) * CAP)
        at = block_of(2 * z + core)
        keep_ref[to] = own_ref[at, :] + far_ref[at, :].astype(F32)
        at = block_of(2 * z + 1 - core)
        give_ref[to] = (own_ref[at, :] + far_ref[at, :].astype(F32)).astype(BF16)


def halves(here, own, far_part):
    rows, width = own.shape
    return pl.pallas_call(
        halves_kernel,
        out_shape=[pltpu.VMEM((rows // 2, width), F32), pltpu.VMEM((rows // 2, width), BF16)],
        in_specs=whole(1, pltpu.SMEM) + whole(2),
        out_specs=whole(2),
        compiler_params=params(),
        cost_estimate=pl.CostEstimate(flops=1_000_000, bytes_accessed=3_000_000, transcendentals=0),
        name="halve_rows",
    )(here, near(own), near(far_part))


def sum_kernel(here_ref, keep_ref, prev_ref, next_ref, given_ref, prev_other_ref, next_other_ref, *out_refs):
    z = here_ref[0] >> 1
    for step, out_ref in enumerate(out_refs):
        at = block_of((z + step) & 3)
        mine = keep_ref[at, :] + prev_ref[at, :].astype(F32) + next_ref[at, :].astype(F32)
        other = given_ref[at, :].astype(F32) + prev_other_ref[at, :].astype(F32) + next_other_ref[at, :].astype(F32)
        out_ref[:CAP] = mine.astype(BF16)
        out_ref[CAP:] = other.astype(BF16)


def sum_rows(here, *parts):
    steps, width = EXPERTS // 2, parts[0].shape[1]
    return pl.pallas_call(
        sum_kernel,
        out_shape=[pltpu.VMEM((2 * CAP, width), BF16)] * steps,
        in_specs=whole(1, pltpu.SMEM) + whole(len(parts)),
        out_specs=whole(steps),
        compiler_params=params(),
        cost_estimate=pl.CostEstimate(flops=1_000_000, bytes_accessed=4_000_000, transcendentals=0),
        name="sum_rows",
    )(here, *(near(p) for p in parts))


def combine_kernel(here_ref, high_ref, low_ref, *refs):
    *block_refs, out_ref, held = refs
    z, core = here_ref[0] >> 1, here_ref[0] & 1
    for step, ref in zip(STEPS, block_refs):
        chip = 2 * ((z - step) & 3)
        held[block_of(chip + core), :] = ref[:CAP]
        held[block_of(chip + 1 - core), :] = ref[CAP:]
    rows = held[...]
    total = jnp.dot(high_ref[...], rows, preferred_element_type=F32)
    total += jnp.dot(low_ref[...], rows, preferred_element_type=F32)
    out_ref[...] = total.astype(BF16)


def combine(here, high, low, blocks):
    tokens, width = high.shape[0], blocks[0].shape[1]
    return pl.pallas_call(
        combine_kernel,
        out_shape=jax.ShapeDtypeStruct((tokens, width), BF16),
        in_specs=whole(1, pltpu.SMEM) + whole(2 + len(blocks)),
        out_specs=pl.BlockSpec(memory_space=pltpu.VMEM),
        scratch_shapes=[pltpu.VMEM((EXPERTS * CAP, width), BF16)],
        compiler_params=params(),
        cost_estimate=pl.CostEstimate(flops=200_000_000, bytes_accessed=1_000_000, transcendentals=0),
        name="combine_rows",
    )(here, near(high), near(low), *(near(b) for b in blocks))


def net_kernel(n_x, pieces, depths, sum_at, add, outs, tile, *refs):
    x_refs, refs = refs[:n_x], refs[n_x:]
    piece_refs, refs = refs[: len(pieces)], refs[len(pieces) :]
    n_sums = len(refs) - max(len(outs), 1) - 3
    if n_sums:
        acc_ref, refs = refs[0], refs[1:]
    if outs:
        out_refs, refs = refs[: len(outs)], refs[len(outs) :]
    else:
        sum_ref, refs = refs[0], refs[1:]
    x, gate_up, down = refs
    rows, width = x.shape
    starts = [sum(depths[:c]) for c in range(len(depths))]

    at = 0
    for ref in x_refs:
        x[at : at + ref.shape[0], :] = ref[...]
        at += ref.shape[0]

    spans, at = [[] for _ in depths], 0
    for ref, (teacher, first, count) in zip(piece_refs, pieces):
        done = 0
        while done < count:
            chunk = max(c for c in range(len(depths)) if starts[c] <= at)
            n = min(count - done, starts[chunk] + depths[chunk] - at)
            spans[chunk].append((ref, teacher, first + done, at - starts[chunk], n))
            at += n
            done += n
    empty = sum(depths) - at

    for c, depth in enumerate(depths):
        low = 2 * starts[c]
        for ref, teacher, first, at, n in spans[c]:
            units = ref.shape[0] // 3
            for k in range(2):
                gate_up[low + k * depth + at : low + k * depth + at + n, :] = ref[k * units + first : k * units + first + n, :]
            part = ref[2 * units + first : 2 * units + first + n, :]
            down[starts[c] + at : starts[c] + at + n, :] = -part if teacher else part
        if empty and c == len(depths) - 1:
            zeros = jnp.zeros((empty, width), BF16)
            for end in (low + depth, low + 2 * depth):
                gate_up[end - empty : end, :] = zeros
            down[starts[c] + depth - empty : starts[c] + depth, :] = zeros

        @pl.loop(0, rows // tile)
        def _(r, c=c, depth=depth, low=low):
            at = pl.ds(pl.multiple_of(r * tile, tile), tile)
            rows_in = x[at, :]
            turned = (((1,), (1,)), ((), ()))
            gate = lax.dot_general(rows_in, gate_up[low : low + depth], turned, preferred_element_type=F32)
            up = lax.dot_general(rows_in, gate_up[low + depth : low + 2 * depth], turned, preferred_element_type=F32)
            hidden = (gate / (1.0 + jnp.exp(-gate)) * up).astype(BF16)
            term = jnp.dot(hidden, down[starts[c] : starts[c] + depth], preferred_element_type=F32)
            within = pl.ds(pl.multiple_of(sum_at + r * tile, tile), tile)
            if not outs and (add or c > 0):
                sum_ref[within, :] += term
            elif not outs:
                sum_ref[within, :] = term
            else:
                term += acc_ref[within, :]
                ends = [sum(n for n, _ in outs[: i + 1]) for i in range(len(outs))]
                for t in range(rows // tile):

                    @pl.when(r == t)
                    def _(t=t):
                        for (n, dtype), end, ref in zip(outs, ends, out_refs):
                            if t * tile < end <= (t + 1) * tile:
                                ref[...] = term[end - n - t * tile : end - t * tile].astype(dtype)


def last_kernel(teacher, sum_at, halved, *refs):
    if halved:
        here_ref, *refs, held = refs
        refs, out_refs = refs[:-4], refs[-4:]
        *refs, sum_ref = refs
    else:
        *refs, sum_ref, out_ref = refs
    x_refs, piece_refs = refs[: -len(teacher)], refs[-len(teacher) :]
    x = x_refs[0][...] if len(x_refs) == 1 else jnp.concatenate([r[...] for r in x_refs], axis=0)
    units = piece_refs[0].shape[0] // 3
    turned = (((1,), (1,)), ((), ()))
    gate = lax.dot_general(x, jnp.concatenate([r[:units] for r in piece_refs], axis=0), turned, preferred_element_type=F32)
    up = lax.dot_general(x, jnp.concatenate([r[units : 2 * units] for r in piece_refs], axis=0), turned, preferred_element_type=F32)
    hidden = (gate / (1.0 + jnp.exp(-gate)) * up).astype(BF16)
    down = jnp.concatenate([-r[2 * units :] if negative else r[2 * units :] for r, negative in zip(piece_refs, teacher)], axis=0)
    total = sum_ref[sum_at : sum_at + x.shape[0], :] + jnp.dot(hidden, down, preferred_element_type=F32)
    if not halved:
        out_ref[...] = total.astype(out_ref.dtype)
        return
    held[...] = total
    for i, out_ref in enumerate(out_refs):
        for z in range(EXPERTS // 2):
            place = EXPERTS * (i // 2) + 2 * z + ((here_ref[0] + i) & 1)
            out_ref[z * CAP : (z + 1) * CAP] = held[block_of(place), :].astype(out_ref.dtype)


def last_net(xs, pieces, total, total_at, dtype, here=None):
    rows, width = sum(a.shape[0] for a in xs), xs[0].shape[1]
    halved = here is not None
    hidden = sum(p.shape[0] // 3 for p, _ in pieces)
    operands = list(xs) + [p for p, _ in pieces] + [total]
    return pl.pallas_call(
        functools.partial(last_kernel, tuple(t for _, t in pieces), total_at, halved),
        out_shape=[pltpu.VMEM((rows // 4, width), dtype)] * 4 if halved else pltpu.VMEM((rows, width), dtype),
        in_specs=(whole(1, pltpu.SMEM) if halved else []) + whole(len(operands)),
        out_specs=whole(4) if halved else whole(1)[0],
        scratch_shapes=[pltpu.VMEM((rows, width), F32)] if halved else [],
        compiler_params=params(),
        cost_estimate=pl.CostEstimate(
            flops=rows * width * hidden * 6, bytes_accessed=rows * width * 8 + hidden * width * 6, transcendentals=rows * hidden
        ),
        name="networks_last",
    )(*([here] if halved else []), *(near(a) for a in operands))


def net(xs, pieces, depths, tile, limit, total, total_at, add, outs=()):
    rows, width = sum(a.shape[0] for a in xs), xs[0].shape[1]
    fresh = isinstance(total, int)
    hidden = sum(depths)
    assert not outs or len(depths) == 1
    operands = list(xs) + [p[0] for p in pieces] + ([] if fresh else [total])
    shapes = outs or [(total if fresh else total.shape[0], F32)]
    return pl.pallas_call(
        functools.partial(net_kernel, len(xs), tuple(p[1:] for p in pieces), tuple(depths), total_at, add, tuple(outs), tile),
        out_shape=[pltpu.VMEM((n, width), d) for n, d in shapes],
        in_specs=whole(len(operands)),
        out_specs=whole(len(shapes)),
        input_output_aliases={} if fresh or outs else {len(operands) - 1: 0},
        scratch_shapes=[
            pltpu.VMEM((rows, width), BF16),
            pltpu.VMEM((2 * hidden, width), BF16),
            pltpu.VMEM((hidden, width), BF16),
        ],
        compiler_params=params(limit),
        cost_estimate=pl.CostEstimate(
            flops=rows * width * hidden * 6, bytes_accessed=rows * width * 8 + hidden * width * 6, transcendentals=rows * hidden
        ),
        name="networks",
    )(*(near(a) for a in operands))


def per_device(tokens, routes, gate_num, student_gate, student_up, student_down, teacher_gate, teacher_up, teacher_down):
    here = lax.axis_index("expert").astype(jnp.int32).reshape(1)
    routes, gate_num = routes.T, gate_num.T
    width = tokens.shape[1]
    units = student_gate.shape[2]
    block = EXPERTS * CAP
    half = block // 2
    mib = 1024 * 1024
    cut = units - 128

    student, rows = pack((student_gate[0], student_up[0], student_down[0]), routes, tokens)
    (teacher,) = pack((teacher_gate[0], teacher_up[0], teacher_down[0]))
    prev_student = send(student, ring(1, True))
    next_teacher = send(teacher, ring(-1, True))
    rows, teacher = barrier(rows, teacher)
    rows = rows.reshape(EXPERTS, CAP, width)
    rows = lax.all_to_all(rows, "expert", split_axis=0, concat_axis=0, tiled=True).reshape(block, width)

    prev_rows = send(rows, ring(1, False))
    next_rows = send(rows, ring(-1, False))
    first = [(student, False, 0, units), (teacher, True, 0, units), (prev_student, False, 0, units), (next_teacher, True, 0, units)]
    (total,) = net([rows], first, [512, 768], block, 28 * mib, 4 * block, 3 * block, False)

    parts = split(cut, barrier(student, total)[0], teacher)
    total, prev_student, next_teacher = barrier(total, prev_student, next_teacher)
    far_student = send(prev_student, ring(1, True))
    far_teacher = send(next_teacher, ring(-1, True))
    total, prev_rows, next_rows, *parts = barrier(total, prev_rows, next_rows, *parts)
    far_a = send(prev_rows[:half], ring(1, False))
    far_b = send(next_rows[half:], ring(-1, False))
    first = [(student, False, 0, units), (teacher, True, 0, units), (prev_student, False, 0, units), (next_teacher, True, 0, units)]
    near_xs = [next_rows, prev_rows]
    (total,) = net(near_xs, first, [512, 768], 2 * block, 32 * mib, total, block, False)

    total, *parts = barrier(total, *parts)
    student_a, student_b, teacher_a, teacher_b = parts
    prev_teacher_a = send(teacher_a, ring(1, True))
    next_student_a = send(student_a, ring(-1, True))
    far_xs = [far_a, far_b]
    (total,) = net(far_xs, first, [512, 768], block, 28 * mib, total, 0, False)
    high, low = shares(routes, gate_num)

    total, far_student, far_teacher, student_b, teacher_b = barrier(total, far_student, far_teacher, student_b, teacher_b)
    room = 512 - units
    second = [(far_student, False, 0, units), (far_teacher, True, 0, room)]
    third = [(far_teacher, True, room, units - room), (prev_teacher_a, True, 0, cut), (next_student_a, False, 0, cut)]
    last = [(send(teacher_b, ring(1, True)), True), (send(student_b, ring(-1, True)), False)]
    (total,) = net(far_xs + near_xs + [rows], second, [512], 2 * block, 24 * mib, total, 0, True)
    (total,) = net(far_xs + near_xs + [rows], third, [512], 2 * block, 24 * mib, total, 0, True)
    far_sum = last_net(far_xs, last, total, 0, BF16)
    total, far_sum = barrier(total, far_sum)
    far_sum = send(far_sum, ring(2, False))
    next_same, next_other, prev_same, prev_other = last_net(near_xs, last, total, block, BF16, here)
    total, _ = barrier(total, next_same)
    prev_part, prev_cross = send(next_same, ring(1, False)), send(next_other, cross(1))
    next_part, next_cross = send(prev_same, ring(-1, False)), send(prev_other, cross(-1))
    own = last_net([rows], last, total, 3 * block, F32)
    keep, give = halves(here, own, far_sum)
    given = send(give, cross(0))
    blocks = sum_rows(here, keep, prev_part, next_part, given, prev_cross, next_cross)
    return combine(here, high, low, [send(blocks[step], along_z(step)) if step else blocks[0] for step in STEPS])


def solution(mesh):
    in_specs = (
        P(("expert", "shard"), None),
        P(("expert", "shard"), None),
        P(("expert", "shard"), None),
        P("expert", None, "shard"),
        P("expert", None, "shard"),
        P("expert", "shard", None),
        P("expert", None, "shard"),
        P("expert", None, "shard"),
        P("expert", "shard", None),
    )
    out_specs = P(("expert", "shard"), None)
    return jax.shard_map(
        per_device, mesh=mesh, in_specs=in_specs, out_specs=out_specs, check_vma=False
    )
```

profile of v0, /device:TPU:1, one launch (start us, length us, event | category | flops | bytes accessed | tf_op | source)
XLA Modules:
  0.0 112.7 jit_solution(12673564296881427380)
XLA Ops:
  0.0 2.5 %pack_weights.2 = (bf16[912,896]{1,0:T(8,128)(2,1)S(1)}, bf16[384,896]{1,0:T(8,128)(2,1)S(1)}) custom-call(bf16[304,896]{1,0:T(8,128)(2,1)} %bitcast.32, bf16[304,896]{1,0:T(8,128)(2,1)} %bitcast.33, bf16[304,896]{1,0:T(8,128)(2,1)} %bitcast.34, s32[2,128]{1,0:T(2,128)} %bitcast.29, bf16[128,896]{1,0:T(8,128)(2,1)} %refs_4_.1), custom_call_target="tpu_custom_call" | custom-call | flops 100000000 | bytes 4000000 | tf_op jit(solution)/shard_map/pack_weights/pallas_call | solution.py:98
  2.5 2.2 %collective-permute-start = (bf16[912,896]{1,0:T(8,128)(2,1)S(1)}, bf16[912,896]{1,0:T(8,128)(2,1)S(1)}, u32[]{:S(2)}, u32[]{:S(2)}) collective-permute-start(bf16[912,896]{1,0:T(8,128)(2,1)S(1)} %get-tuple-element.56.refs_1_.refs_0_.refs_2_), channel_id=1, source_target_pairs={{0,1},{1,2},{2,3},{3,0},{4,5},{5,6},{6,7},{7,4},{8,9},{9,10},{10,1... | collective-permute-start | bytes 4902920 | tf_op jit(solution)/shard_map/ppermute | solution.py:42
  4.7 0.0 copy-done.4
  4.7 0.2 pack_weights.3.refs_2_.refs_1_.refs_3_
  4.9 1.5 %collective-permute-start.1 = (bf16[912,896]{1,0:T(8,128)(2,1)S(1)}, bf16[912,896]{1,0:T(8,128)(2,1)S(1)}, u32[]{:S(2)}, u32[]{:S(2)}) collective-permute-start(bf16[912,896]{1,0:T(8,128)(2,1)S(1)} %pack_weights.3.refs_2_.refs_1_.refs_3_), channel_id=1, source_target_pairs={{0,3},{1,0},{2,1},{3,2},{4,7},{5,4},{6,5},{7,6},{8,11},{9,8},{10,9... | collective-permute-start | bytes 4902920 | tf_op jit(solution)/shard_map/ppermute | solution.py:42
  6.5 17.5 %all_to_all.5 = bf16[8,48,896]{2,1,0:T(8,128)(2,1)S(1)} all-to-all(bf16[8,48,896]{2,1,0:T(8,128)(2,1)S(1)} %bitcast.25), channel_id=1, replica_groups=mesh['expert'=8,'shard'=16] {'expert'}, dimensions={0} | all-to-all | bytes 1376256 | tf_op jit(solution)/shard_map/all_to_all | solution.py:391
  24.0 0.2 collective-permute-start.2
  24.1 2.5 %collective-permute-start.3 = (bf16[384,896]{1,0:T(8,128)(2,1)S(1)}, bf16[384,896]{1,0:T(8,128)(2,1)S(1)}, u32[]{:S(2)}, u32[]{:S(2)}) collective-permute-start(bf16[384,896]{1,0:T(8,128)(2,1)S(1)} %bitcast.20), channel_id=1, source_target_pairs={{0,12},{1,13},{2,14},{3,15},{4,0},{5,1},{6,2},{7,3},{8,4},{9,5},{1... | collective-permute-start | bytes 2064392 | tf_op jit(solution)/shard_map/ppermute | solution.py:42
  26.6 0.0 collective-permute-done.refs_3_.refs_4_
  26.6 0.0 collective-permute-done.1.refs_4_.refs_5_
  26.6 3.4 %networks.5.refs_6_ = f32[1536,896]{1,0:T(8,128)S(1)} custom-call(bf16[384,896]{1,0:T(8,128)(2,1)S(1)} %bitcast.21, bf16[912,896]{1,0:T(8,128)(2,1)S(1)} %get-tuple-element.56.refs_1_.refs_0_.refs_2_, bf16[912,896]{1,0:T(8,128)(2,1)S(1)} %pack_weights.3.refs_2_.refs_1_.refs_3_, bf16[912,896]{1,0:T(8,128)(2,1)S(1)} %collective-permute-done.refs_3_.refs_4_, ...), custom_call_target="tpu_custom_call" | custom-call | flops 2642411520 | bytes 9633792 | tf_op jit(solution)/shard_map/networks/pallas_call | solution.py:356
  30.1 1.4 %collective-permute-start.6 = (bf16[912,896]{1,0:T(8,128)(2,1)S(1)}, bf16[912,896]{1,0:T(8,128)(2,1)S(1)}, u32[]{:S(2)}, u32[]{:S(2)}) collective-permute-start(bf16[912,896]{1,0:T(8,128)(2,1)S(1)} %collective-permute-done.refs_3_.refs_4_), channel_id=1, source_target_pairs={{0,1},{1,2},{2,3},{3,0},{4,5},{5,6},{6,7},{7,4},{8,9},{9,10},{10,1... | collective-permute-start | bytes 4902920 | tf_op jit(solution)/shard_map/ppermute | solution.py:42
  31.4 1.5 %collective-permute-start.7 = (bf16[912,896]{1,0:T(8,128)(2,1)S(1)}, bf16[912,896]{1,0:T(8,128)(2,1)S(1)}, u32[]{:S(2)}, u32[]{:S(2)}) collective-permute-start(bf16[912,896]{1,0:T(8,128)(2,1)S(1)} %collective-permute-done.1.refs_4_.refs_5_), channel_id=1, source_target_pairs={{0,3},{1,0},{2,1},{3,2},{4,7},{5,4},{6,5},{7,6},{8,11},{9,8},{10,9... | collective-permute-start | bytes 4902920 | tf_op jit(solution)/shard_map/ppermute | solution.py:42
  32.9 0.2 split_weights.1
  33.2 2.1 %collective-permute-done.2.refs_1_.refs_3_.refs_2_ = bf16[384,896]{1,0:T(8,128)(2,1)S(1)} collective-permute-done((bf16[384,896]{1,0:T(8,128)(2,1)S(1)}, bf16[384,896]{1,0:T(8,128)(2,1)S(1)}, u32[]{:S(2)}, u32[]{:S(2)}) %collective-permute-start.2) | collective-permute-done | bytes 688160 | tf_op jit(solution)/shard_map/ppermute | solution.py:42
  35.2 0.0 collective-permute-done.3.refs_0_.refs_2_.refs_1_
  35.3 0.3 collective-permute-start.4
  35.6 2.6 %collective-permute-start.5 = (bf16[192,896]{1,0:T(8,128)(2,1)S(1)}, bf16[192,896]{1,0:T(8,128)(2,1)S(1)}, u32[]{:S(2)}, u32[]{:S(2)}) collective-permute-start(bf16[192,896]{1,0:T(8,128)(2,1)S(1)} %slice.7), channel_id=1, source_target_pairs={{0,12},{1,13},{2,14},{3,15},{4,0},{5,1},{6,2},{7,3},{8,4},{9,5},{1... | collective-permute-start | bytes 1032200 | tf_op jit(solution)/shard_map/ppermute | solution.py:42
  38.1 6.5 %networks.6.refs_6_ = f32[1536,896]{1,0:T(8,128)S(1)} custom-call(bf16[384,896]{1,0:T(8,128)(2,1)S(1)} %collective-permute-done.3.refs_0_.refs_2_.refs_1_, bf16[384,896]{1,0:T(8,128)(2,1)S(1)} %collective-permute-done.2.refs_1_.refs_3_.refs_2_, bf16[912,896]{1,0:T(8,128)(2,1)S(1)} %get-tuple-element.56.refs_1_.refs_0_.refs_2_, ...), custom_call_target="tpu_custom_call", output_to_operand_aliasing={{}: (6, {})} | custom-call | flops 5284823040 | bytes 12386304 | tf_op jit(solution)/shard_map/networks/pallas_call | solution.py:356
  44.7 1.9 %collective-permute-start.10 = (bf16[528,896]{1,0:T(8,128)(2,1)S(1)}, bf16[528,896]{1,0:T(8,128)(2,1)S(1)}, u32[]{:S(2)}, u32[]{:S(2)}) collective-permute-start(bf16[528,896]{1,0:T(8,128)(2,1)S(1)} %get-tuple-element.76), channel_id=1, source_target_pairs={{0,1},{1,2},{2,3},{3,0},{4,5},{5,6},{6,7},{7,4},{8,9},{9,10},{10,1... | collective-permute-start | bytes 2838536 | tf_op jit(solution)/shard_map/ppermute | solution.py:42
  46.6 0.1 collective-permute-done.4.refs_0_
  46.7 3.1 %collective-permute-start.11 = (bf16[528,896]{1,0:T(8,128)(2,1)S(1)}, bf16[528,896]{1,0:T(8,128)(2,1)S(1)}, u32[]{:S(2)}, u32[]{:S(2)}) collective-permute-start(bf16[528,896]{1,0:T(8,128)(2,1)S(1)} %get-tuple-element.77), channel_id=1, source_target_pairs={{0,3},{1,0},{2,1},{3,2},{4,7},{5,4},{6,5},{7,6},{8,11},{9,8},{10,9... | collective-permute-start | bytes 2838536 | tf_op jit(solution)/shard_map/ppermute | solution.py:42
  49.8 0.0 collective-permute-done.5.refs_1_
  49.8 3.4 %networks.7.refs_7_ = f32[1536,896]{1,0:T(8,128)S(1)} custom-call(bf16[192,896]{1,0:T(8,128)(2,1)S(1)} %collective-permute-done.4.refs_0_, bf16[192,896]{1,0:T(8,128)(2,1)S(1)} %collective-permute-done.5.refs_1_, bf16[912,896]{1,0:T(8,128)(2,1)S(1)} %get-tuple-element.56.refs_1_.refs_0_.refs_2_, ...), custom_call_target="tpu_custom_call", output_to_operand_aliasing={{}: (6, {})} | custom-call | flops 2642411520 | bytes 9633792 | tf_op jit(solution)/shard_map/networks/pallas_call | solution.py:356
  53.2 4.6 %collective-permute-done.6.refs_5_ = bf16[912,896]{1,0:T(8,128)(2,1)S(1)} collective-permute-done((bf16[912,896]{1,0:T(8,128)(2,1)S(1)}, bf16[912,896]{1,0:T(8,128)(2,1)S(1)}, u32[]{:S(2)}, u32[]{:S(2)}) %collective-permute-start.6) | collective-permute-done | bytes 1634336 | tf_op jit(solution)/shard_map/ppermute | solution.py:42
  57.8 0.4 collective-permute-done.7.refs_6_.refs_5_
  58.2 1.3 %collective-permute-start.8 = (bf16[384,896]{1,0:T(8,128)(2,1)S(1)}, bf16[384,896]{1,0:T(8,128)(2,1)S(1)}, u32[]{:S(2)}, u32[]{:S(2)}) collective-permute-start(bf16[384,896]{1,0:T(8,128)(2,1)S(1)} %get-tuple-element.73), channel_id=1, source_target_pairs={{0,1},{1,2},{2,3},{3,0},{4,5},{5,6},{6,7},{7,4},{8,9},{9,10},{10,1... | collective-permute-start | bytes 2064392 | tf_op jit(solution)/shard_map/ppermute | solution.py:42
  59.5 1.4 %collective-permute-start.9 = (bf16[384,896]{1,0:T(8,128)(2,1)S(1)}, bf16[384,896]{1,0:T(8,128)(2,1)S(1)}, u32[]{:S(2)}, u32[]{:S(2)}) collective-permute-start(bf16[384,896]{1,0:T(8,128)(2,1)S(1)} %get-tuple-element.74), channel_id=1, source_target_pairs={{0,3},{1,0},{2,1},{3,2},{4,7},{5,4},{6,5},{7,6},{8,11},{9,8},{10,9... | collective-permute-start | bytes 2064392 | tf_op jit(solution)/shard_map/ppermute | solution.py:42
  60.9 5.7 %networks.8.refs_8_ = f32[1536,896]{1,0:T(8,128)S(1)} custom-call(bf16[192,896]{1,0:T(8,128)(2,1)S(1)} %collective-permute-done.4.refs_0_, bf16[192,896]{1,0:T(8,128)(2,1)S(1)} %collective-permute-done.5.refs_1_, bf16[384,896]{1,0:T(8,128)(2,1)S(1)} %collective-permute-done.3.refs_0_.refs_2_.refs_1_, ...), custom_call_target="tpu_custom_call", output_to_operand_aliasing={{}: (7, {})} | custom-call | flops 4227858432 | bytes 13762560 | tf_op jit(solution)/shard_map/networks/pallas_call | solution.py:356
  66.6 1.4 %collective-permute-done.10.refs_6_ = bf16[528,896]{1,0:T(8,128)(2,1)S(1)} collective-permute-done((bf16[528,896]{1,0:T(8,128)(2,1)S(1)}, bf16[528,896]{1,0:T(8,128)(2,1)S(1)}, u32[]{:S(2)}, u32[]{:S(2)}) %collective-permute-start.10) | collective-permute-done | bytes 946208 | tf_op jit(solution)/shard_map/ppermute | solution.py:42
  68.0 0.4 collective-permute-done.11.refs_7_
  68.3 5.7 %networks.9.refs_4_.refs_5_.refs_3_ = f32[1536,896]{1,0:T(8,128)S(1)} custom-call(bf16[192,896]{1,0:T(8,128)(2,1)S(1)} %collective-permute-done.4.refs_0_, bf16[192,896]{1,0:T(8,128)(2,1)S(1)} %collective-permute-done.5.refs_1_, bf16[384,896]{1,0:T(8,128)(2,1)S(1)} %collective-permute-done.3.refs_0_.refs_2_.refs_1_, ...), custom_call_target="tpu_custom_call", output_to_operand_aliasing={{}: (8, {})} | custom-call | flops 4227858432 | bytes 13762560 | tf_op jit(solution)/shard_map/networks/pallas_call | solution.py:356
  74.1 0.0 copy-start
  74.1 1.0 collective-permute-done.8.refs_2_.refs_3_.refs_1_
  75.0 0.4 collective-permute-done.9.refs_3_.refs_4_.refs_2_
  75.4 1.7 %networks_last.3 = bf16[384,896]{1,0:T(8,128)(2,1)} custom-call(bf16[192,896]{1,0:T(8,128)(2,1)S(1)} %collective-permute-done.4.refs_0_, bf16[192,896]{1,0:T(8,128)(2,1)S(1)} %collective-permute-done.5.refs_1_, bf16[384,896]{1,0:T(8,128)(2,1)S(1)} %collective-permute-done.8.refs_2_.refs_3_.refs_1_, ...), custom_call_target="tpu_custom_call" | custom-call | flops 528482304 | bytes 4128768 | tf_op jit(solution)/shard_map/networks_last/pallas_call | solution.py:335
  77.1 1.5 %collective-permute-start.12 = (bf16[384,896]{1,0:T(8,128)(2,1)}, bf16[384,896]{1,0:T(8,128)(2,1)}, u32[]{:S(2)}, u32[]{:S(2)}) collective-permute-start(bf16[384,896]{1,0:T(8,128)(2,1)} %networks_last.3), channel_id=1, source_target_pairs={{0,8},{1,9},{2,10},{3,11},{4,12},{5,13},{6,14},{7,15},{8,0},{9,1},... | collective-permute-start | bytes 2064392 | tf_op jit(solution)/shard_map/ppermute | solution.py:42
  78.7 2.6 %copy-done.1 = f32[1536,896]{1,0:T(8,128)S(1)} copy-done((f32[1536,896]{1,0:T(8,128)S(1)}, f32[1536,896]{1,0:T(8,128)}, u32[]{:S(2)}) %copy-start.1) | copy-done | bytes 5505048
  81.2 1.8 %networks_last.4 = (bf16[192,896]{1,0:T(8,128)(2,1)S(1)}, bf16[192,896]{1,0:T(8,128)(2,1)S(1)}, bf16[192,896]{1,0:T(8,128)(2,1)S(1)}, bf16[192,896]{1,0:T(8,128)(2,1)S(1)}) custom-call(s32[1]{0:T(128)} %bitcast.refs_0_.here_ref, bf16[384,896]{1,0:T(8,128)(2,1)S(1)} %collective-permute-done.3.refs_0_.refs_2_.refs_1_, ...), custom_call_target="tpu_custom_call" | custom-call | flops 1056964608 | bytes 6881280 | tf_op jit(solution)/shard_map/networks_last/pallas_call | solution.py:335
  83.0 0.7 collective-permute-start.13
  83.7 2.1 %collective-permute-start.14 = (bf16[192,896]{1,0:T(8,128)(2,1)S(1)}, bf16[192,896]{1,0:T(8,128)(2,1)S(1)}, u32[]{:S(2)}, u32[]{:S(2)}) collective-permute-start(bf16[192,896]{1,0:T(8,128)(2,1)S(1)} %get-tuple-element.85), channel_id=1, source_target_pairs={{0,12},{1,13},{2,14},{3,15},{4,0},{5,1},{6,2},{7,3},{8,4},{9,5},{1... | collective-permute-start | bytes 1032200 | tf_op jit(solution)/shard_map/ppermute | solution.py:42
  85.8 1.8 %collective-permute-start.16 = (bf16[192,896]{1,0:T(8,128)(2,1)S(1)}, bf16[192,896]{1,0:T(8,128)(2,1)S(1)}, u32[]{:S(2)}, u32[]{:S(2)}) collective-permute-start(bf16[192,896]{1,0:T(8,128)(2,1)S(1)} %get-tuple-element.87), channel_id=1, source_target_pairs={{0,20},{1,21},{2,22},{3,23},{4,24},{5,25},{6,26},{7,27},{8,28},{9,... | collective-permute-start | bytes 1032200 | tf_op jit(solution)/shard_map/ppermute | solution.py:42
  87.6 1.9 %collective-permute-start.17 = (bf16[192,896]{1,0:T(8,128)(2,1)S(1)}, bf16[192,896]{1,0:T(8,128)(2,1)S(1)}, u32[]{:S(2)}, u32[]{:S(2)}) collective-permute-start(bf16[192,896]{1,0:T(8,128)(2,1)S(1)} %get-tuple-element.88), channel_id=1, source_target_pairs={{0,28},{1,29},{2,30},{3,31},{4,16},{5,17},{6,18},{7,19},{8,20},{9,... | collective-permute-start | bytes 1032200 | tf_op jit(solution)/shard_map/ppermute | solution.py:42
  89.5 0.9 networks_last.5.own_ref
  90.4 0.0 collective-permute-done.12.far_ref
  90.4 1.2 %halve_rows.1 = (f32[192,896]{1,0:T(8,128)S(1)}, bf16[192,896]{1,0:T(8,128)(2,1)S(1)}) custom-call(s32[1]{0:T(128)} %bitcast.refs_0_.here_ref, f32[384,896]{1,0:T(8,128)S(1)} %networks_last.5.own_ref, bf16[384,896]{1,0:T(8,128)(2,1)} %collective-permute-done.12.far_ref), custom_call_target="tpu_custom_call" | custom-call | flops 1000000 | bytes 3000000 | tf_op jit(solution)/shard_map/halve_rows/pallas_call | solution.py:173
  91.7 0.0 copy-start.6
  91.7 0.0 copy-start.7
  91.7 0.1 collective-permute-start.15
  91.8 0.9 collective-permute-done.13.prev_ref
  92.6 0.0 collective-permute-done.14.next_ref
  92.6 3.7 %collective-permute-done.16.prev_other_ref = bf16[192,896]{1,0:T(8,128)(2,1)S(1)} collective-permute-done((bf16[192,896]{1,0:T(8,128)(2,1)S(1)}, bf16[192,896]{1,0:T(8,128)(2,1)S(1)}, u32[]{:S(2)}, u32[]{:S(2)}) %collective-permute-start.16) | collective-permute-done | bytes 344096 | tf_op jit(solution)/shard_map/ppermute | solution.py:42
  96.3 0.0 collective-permute-done.17.next_other_ref
  96.3 0.0 collective-permute-done.15.given_ref
  96.3 0.2 sum_rows.1
  96.6 5.6 %collective-permute-start.18 = (bf16[96,896]{1,0:T(8,128)(2,1)S(1)}, bf16[96,896]{1,0:T(8,128)(2,1)S(1)}, u32[]{:S(2)}, u32[]{:S(2)}) collective-permute-start(bf16[96,896]{1,0:T(8,128)(2,1)S(1)} %get-tuple-element.89), channel_id=1, source_target_pairs={{0,64},{1,65},{2,66},{3,67},{4,68},{5,69},{6,70},{7,71},{8,72},{9,... | collective-permute-start | bytes 516104 | tf_op jit(solution)/shard_map/ppermute | solution.py:42
  102.2 0.7 collective-permute-start.19
  103.0 1.9 %collective-permute-start.20 = (bf16[96,896]{1,0:T(8,128)(2,1)S(1)}, bf16[96,896]{1,0:T(8,128)(2,1)S(1)}, u32[]{:S(2)}, u32[]{:S(2)}) collective-permute-start(bf16[96,896]{1,0:T(8,128)(2,1)S(1)} %get-tuple-element.91), channel_id=1, source_target_pairs={{0,96},{1,97},{2,98},{3,99},{4,100},{5,101},{6,102},{7,103},{8,104... | collective-permute-start | bytes 516104 | tf_op jit(solution)/shard_map/ppermute | solution.py:42
  104.9 0.0 copy-done.7
  104.9 0.3 gate_shares.1
  105.2 1.7 %collective-permute-done.18.refs_0_ = bf16[96,896]{1,0:T(8,128)(2,1)S(1)} collective-permute-done((bf16[96,896]{1,0:T(8,128)(2,1)S(1)}, bf16[96,896]{1,0:T(8,128)(2,1)S(1)}, u32[]{:S(2)}, u32[]{:S(2)}) %collective-permute-start.18) | collective-permute-done | bytes 172064 | tf_op jit(solution)/shard_map/ppermute | solution.py:42
  106.9 3.8 %collective-permute-done.19.refs_1_ = bf16[96,896]{1,0:T(8,128)(2,1)S(1)} collective-permute-done((bf16[96,896]{1,0:T(8,128)(2,1)S(1)}, bf16[96,896]{1,0:T(8,128)(2,1)S(1)}, u32[]{:S(2)}, u32[]{:S(2)}) %collective-permute-start.19) | collective-permute-done | bytes 172064 | tf_op jit(solution)/shard_map/ppermute | solution.py:42
  110.7 0.8 collective-permute-done.20.refs_2_
  111.4 1.2 %combine_rows.1 = bf16[128,896]{1,0:T(8,128)(2,1)} custom-call(s32[1]{0:T(128)} %bitcast.refs_0_.here_ref, bf16[128,384]{1,0:T(8,128)(2,1)S(1)} %get-tuple-element.49.high_ref, bf16[128,384]{1,0:T(8,128)(2,1)S(1)} %get-tuple-element.50.low_ref, bf16[96,896]{1,0:T(8,128)(2,1)S(1)} %collective-permute-done.18.refs_0_, ...), custom_call_target="tpu_custom_call" | custom-call | flops 200000000 | bytes 1000000 | tf_op jit(solution)/shard_map/combine_rows/pallas_call | solution.py:222
  (12 shorter events, 0.1 us)
Async XLA Ops:
  0.0 4.7 %copy-start.4 = (bf16[1,896,304]{1,2,0:T(8,128)(2,1)S(1)}, bf16[1,896,304]{1,2,0:T(8,128)(2,1)}, u32[]{:S(2)}) copy-start(bf16[1,896,304]{1,2,0:T(8,128)(2,1)} %param.16) | copy-start | bytes 1634308
  0.0 4.7 %copy-start.5 = (bf16[1,304,896]{2,1,0:T(8,128)(2,1)S(1)}, bf16[1,304,896]{2,1,0:T(8,128)(2,1)}, u32[]{:S(2)}) copy-start(bf16[1,304,896]{2,1,0:T(8,128)(2,1)} %param.17) | copy-start | bytes 1634308
  0.0 4.7 %copy-start.3 = (bf16[1,896,304]{1,2,0:T(8,128)(2,1)S(1)}, bf16[1,896,304]{1,2,0:T(8,128)(2,1)}, u32[]{:S(2)}) copy-start(bf16[1,896,304]{1,2,0:T(8,128)(2,1)} %param.15) | copy-start | bytes 1634308
  2.5 24.1 %collective-permute-start = (bf16[912,896]{1,0:T(8,128)(2,1)S(1)}, bf16[912,896]{1,0:T(8,128)(2,1)S(1)}, u32[]{:S(2)}, u32[]{:S(2)}) collective-permute-start(bf16[912,896]{1,0:T(8,128)(2,1)S(1)} %get-tuple-element.56.refs_1_.refs_0_.refs_2_), channel_id=1, source_target_pairs={{0,1},{1,2},{2,3},{3,0},{4,5},{5,6},{6,7},{7,4},{8,9},{9,10},{10,1... | collective-permute-start | bytes 4902920 | tf_op jit(solution)/shard_map/ppermute | solution.py:42
  4.9 21.7 %collective-permute-start.1 = (bf16[912,896]{1,0:T(8,128)(2,1)S(1)}, bf16[912,896]{1,0:T(8,128)(2,1)S(1)}, u32[]{:S(2)}, u32[]{:S(2)}) collective-permute-start(bf16[912,896]{1,0:T(8,128)(2,1)S(1)} %pack_weights.3.refs_2_.refs_1_.refs_3_), channel_id=1, source_target_pairs={{0,3},{1,0},{2,1},{3,2},{4,7},{5,4},{6,5},{7,6},{8,11},{9,8},{10,9... | collective-permute-start | bytes 4902920 | tf_op jit(solution)/shard_map/ppermute | solution.py:42
  24.0 11.3 %collective-permute-start.2 = (bf16[384,896]{1,0:T(8,128)(2,1)S(1)}, bf16[384,896]{1,0:T(8,128)(2,1)S(1)}, u32[]{:S(2)}, u32[]{:S(2)}) collective-permute-start(bf16[384,896]{1,0:T(8,128)(2,1)S(1)} %bitcast.19), channel_id=1, source_target_pairs={{0,4},{1,5},{2,6},{3,7},{4,8},{5,9},{6,10},{7,11},{8,12},{9,13},{1... | collective-permute-start | bytes 2064392 | tf_op jit(solution)/shard_map/ppermute | solution.py:42
  24.1 11.1 %collective-permute-start.3 = (bf16[384,896]{1,0:T(8,128)(2,1)S(1)}, bf16[384,896]{1,0:T(8,128)(2,1)S(1)}, u32[]{:S(2)}, u32[]{:S(2)}) collective-permute-start(bf16[384,896]{1,0:T(8,128)(2,1)S(1)} %bitcast.20), channel_id=1, source_target_pairs={{0,12},{1,13},{2,14},{3,15},{4,0},{5,1},{6,2},{7,3},{8,4},{9,5},{1... | collective-permute-start | bytes 2064392 | tf_op jit(solution)/shard_map/ppermute | solution.py:42
  30.1 27.8 %collective-permute-start.6 = (bf16[912,896]{1,0:T(8,128)(2,1)S(1)}, bf16[912,896]{1,0:T(8,128)(2,1)S(1)}, u32[]{:S(2)}, u32[]{:S(2)}) collective-permute-start(bf16[912,896]{1,0:T(8,128)(2,1)S(1)} %collective-permute-done.refs_3_.refs_4_), channel_id=1, source_target_pairs={{0,1},{1,2},{2,3},{3,0},{4,5},{5,6},{6,7},{7,4},{8,9},{9,10},{10,1... | collective-permute-start | bytes 4902920 | tf_op jit(solution)/shard_map/ppermute | solution.py:42
  31.4 26.8 %collective-permute-start.7 = (bf16[912,896]{1,0:T(8,128)(2,1)S(1)}, bf16[912,896]{1,0:T(8,128)(2,1)S(1)}, u32[]{:S(2)}, u32[]{:S(2)}) collective-permute-start(bf16[912,896]{1,0:T(8,128)(2,1)S(1)} %collective-permute-done.1.refs_4_.refs_5_), channel_id=1, source_target_pairs={{0,3},{1,0},{2,1},{3,2},{4,7},{5,4},{6,5},{7,6},{8,11},{9,8},{10,9... | collective-permute-start | bytes 4902920 | tf_op jit(solution)/shard_map/ppermute | solution.py:42
  35.3 11.4 %collective-permute-start.4 = (bf16[192,896]{1,0:T(8,128)(2,1)S(1)}, bf16[192,896]{1,0:T(8,128)(2,1)S(1)}, u32[]{:S(2)}, u32[]{:S(2)}) collective-permute-start(bf16[192,896]{1,0:T(8,128)(2,1)S(1)} %slice.6), channel_id=1, source_target_pairs={{0,4},{1,5},{2,6},{3,7},{4,8},{5,9},{6,10},{7,11},{8,12},{9,13},{1... | collective-permute-start | bytes 1032200 | tf_op jit(solution)/shard_map/ppermute | solution.py:42
  35.6 14.2 %collective-permute-start.5 = (bf16[192,896]{1,0:T(8,128)(2,1)S(1)}, bf16[192,896]{1,0:T(8,128)(2,1)S(1)}, u32[]{:S(2)}, u32[]{:S(2)}) collective-permute-start(bf16[192,896]{1,0:T(8,128)(2,1)S(1)} %slice.7), channel_id=1, source_target_pairs={{0,12},{1,13},{2,14},{3,15},{4,0},{5,1},{6,2},{7,3},{8,4},{9,5},{1... | collective-permute-start | bytes 1032200 | tf_op jit(solution)/shard_map/ppermute | solution.py:42
  44.7 23.3 %collective-permute-start.10 = (bf16[528,896]{1,0:T(8,128)(2,1)S(1)}, bf16[528,896]{1,0:T(8,128)(2,1)S(1)}, u32[]{:S(2)}, u32[]{:S(2)}) collective-permute-start(bf16[528,896]{1,0:T(8,128)(2,1)S(1)} %get-tuple-element.76), channel_id=1, source_target_pairs={{0,1},{1,2},{2,3},{3,0},{4,5},{5,6},{6,7},{7,4},{8,9},{9,10},{10,1... | collective-permute-start | bytes 2838536 | tf_op jit(solution)/shard_map/ppermute | solution.py:42
  46.7 21.6 %collective-permute-start.11 = (bf16[528,896]{1,0:T(8,128)(2,1)S(1)}, bf16[528,896]{1,0:T(8,128)(2,1)S(1)}, u32[]{:S(2)}, u32[]{:S(2)}) collective-permute-start(bf16[528,896]{1,0:T(8,128)(2,1)S(1)} %get-tuple-element.77), channel_id=1, source_target_pairs={{0,3},{1,0},{2,1},{3,2},{4,7},{5,4},{6,5},{7,6},{8,11},{9,8},{10,9... | collective-permute-start | bytes 2838536 | tf_op jit(solution)/shard_map/ppermute | solution.py:42
  58.2 16.9 %collective-permute-start.8 = (bf16[384,896]{1,0:T(8,128)(2,1)S(1)}, bf16[384,896]{1,0:T(8,128)(2,1)S(1)}, u32[]{:S(2)}, u32[]{:S(2)}) collective-permute-start(bf16[384,896]{1,0:T(8,128)(2,1)S(1)} %get-tuple-element.73), channel_id=1, source_target_pairs={{0,1},{1,2},{2,3},{3,0},{4,5},{5,6},{6,7},{7,4},{8,9},{9,10},{10,1... | collective-permute-start | bytes 2064392 | tf_op jit(solution)/shard_map/ppermute | solution.py:42
  59.5 15.9 %collective-permute-start.9 = (bf16[384,896]{1,0:T(8,128)(2,1)S(1)}, bf16[384,896]{1,0:T(8,128)(2,1)S(1)}, u32[]{:S(2)}, u32[]{:S(2)}) collective-permute-start(bf16[384,896]{1,0:T(8,128)(2,1)S(1)} %get-tuple-element.74), channel_id=1, source_target_pairs={{0,3},{1,0},{2,1},{3,2},{4,7},{5,4},{6,5},{7,6},{8,11},{9,8},{10,9... | collective-permute-start | bytes 2064392 | tf_op jit(solution)/shard_map/ppermute | solution.py:42
  74.1 3.1 %copy-start = (f32[1536,896]{1,0:T(8,128)}, f32[1536,896]{1,0:T(8,128)S(1)}, u32[]{:S(2)}) copy-start(f32[1536,896]{1,0:T(8,128)S(1)} %networks.9.refs_4_.refs_5_.refs_3_) | copy-start | bytes 16515076
  77.1 13.3 %collective-permute-start.12 = (bf16[384,896]{1,0:T(8,128)(2,1)}, bf16[384,896]{1,0:T(8,128)(2,1)}, u32[]{:S(2)}, u32[]{:S(2)}) collective-permute-start(bf16[384,896]{1,0:T(8,128)(2,1)} %networks_last.3), channel_id=1, source_target_pairs={{0,8},{1,9},{2,10},{3,11},{4,12},{5,13},{6,14},{7,15},{8,0},{9,1},... | collective-permute-start | bytes 2064392 | tf_op jit(solution)/shard_map/ppermute | solution.py:42
  78.7 2.6 %copy-start.1 = (f32[1536,896]{1,0:T(8,128)S(1)}, f32[1536,896]{1,0:T(8,128)}, u32[]{:S(2)}) copy-start(f32[1536,896]{1,0:T(8,128)} %copy-done) | copy-start | bytes 16515076
  81.2 8.3 %copy-start.2 = (f32[1536,896]{1,0:T(8,128)S(1)}, f32[1536,896]{1,0:T(8,128)}, u32[]{:S(2)}) copy-start(f32[1536,896]{1,0:T(8,128)} %copy-done) | copy-start | bytes 16515076
  83.0 9.6 %collective-permute-start.13 = (bf16[192,896]{1,0:T(8,128)(2,1)S(1)}, bf16[192,896]{1,0:T(8,128)(2,1)S(1)}, u32[]{:S(2)}, u32[]{:S(2)}) collective-permute-start(bf16[192,896]{1,0:T(8,128)(2,1)S(1)} %get-tuple-element.81), channel_id=1, source_target_pairs={{0,4},{1,5},{2,6},{3,7},{4,8},{5,9},{6,10},{7,11},{8,12},{9,13},{1... | collective-permute-start | bytes 1032200 | tf_op jit(solution)/shard_map/ppermute | solution.py:42
  83.7 8.9 %collective-permute-start.14 = (bf16[192,896]{1,0:T(8,128)(2,1)S(1)}, bf16[192,896]{1,0:T(8,128)(2,1)S(1)}, u32[]{:S(2)}, u32[]{:S(2)}) collective-permute-start(bf16[192,896]{1,0:T(8,128)(2,1)S(1)} %get-tuple-element.85), channel_id=1, source_target_pairs={{0,12},{1,13},{2,14},{3,15},{4,0},{5,1},{6,2},{7,3},{8,4},{9,5},{1... | collective-permute-start | bytes 1032200 | tf_op jit(solution)/shard_map/ppermute | solution.py:42
  85.8 10.5 %collective-permute-start.16 = (bf16[192,896]{1,0:T(8,128)(2,1)S(1)}, bf16[192,896]{1,0:T(8,128)(2,1)S(1)}, u32[]{:S(2)}, u32[]{:S(2)}) collective-permute-start(bf16[192,896]{1,0:T(8,128)(2,1)S(1)} %get-tuple-element.87), channel_id=1, source_target_pairs={{0,20},{1,21},{2,22},{3,23},{4,24},{5,25},{6,26},{7,27},{8,28},{9,... | collective-permute-start | bytes 1032200 | tf_op jit(solution)/shard_map/ppermute | solution.py:42
  87.6 8.7 %collective-permute-start.17 = (bf16[192,896]{1,0:T(8,128)(2,1)S(1)}, bf16[192,896]{1,0:T(8,128)(2,1)S(1)}, u32[]{:S(2)}, u32[]{:S(2)}) collective-permute-start(bf16[192,896]{1,0:T(8,128)(2,1)S(1)} %get-tuple-element.88), channel_id=1, source_target_pairs={{0,28},{1,29},{2,30},{3,31},{4,16},{5,17},{6,18},{7,19},{8,20},{9,... | collective-permute-start | bytes 1032200 | tf_op jit(solution)/shard_map/ppermute | solution.py:42
  91.7 13.2 %copy-start.6 = (s32[128,2]{0,1:T(2,128)S(1)}, s32[128,2]{0,1:T(2,128)}, u32[]{:S(2)}) copy-start(s32[128,2]{0,1:T(2,128)} %param.10) | copy-start | bytes 3076
  91.7 13.2 %copy-start.7 = (s32[128,2]{0,1:T(2,128)S(1)}, s32[128,2]{0,1:T(2,128)}, u32[]{:S(2)}) copy-start(s32[128,2]{0,1:T(2,128)} %param.11) | copy-start | bytes 3076
  91.7 4.6 %collective-permute-start.15 = (bf16[192,896]{1,0:T(8,128)(2,1)S(1)}, bf16[192,896]{1,0:T(8,128)(2,1)S(1)}, u32[]{:S(2)}, u32[]{:S(2)}) collective-permute-start(bf16[192,896]{1,0:T(8,128)(2,1)S(1)} %get-tuple-element.86), channel_id=1, source_target_pairs={{0,16},{1,17},{2,18},{3,19},{4,20},{5,21},{6,22},{7,23},{8,24},{9,... | collective-permute-start | bytes 1032200 | tf_op jit(solution)/shard_map/ppermute | solution.py:42
  96.6 10.3 %collective-permute-start.18 = (bf16[96,896]{1,0:T(8,128)(2,1)S(1)}, bf16[96,896]{1,0:T(8,128)(2,1)S(1)}, u32[]{:S(2)}, u32[]{:S(2)}) collective-permute-start(bf16[96,896]{1,0:T(8,128)(2,1)S(1)} %get-tuple-element.89), channel_id=1, source_target_pairs={{0,64},{1,65},{2,66},{3,67},{4,68},{5,69},{6,70},{7,71},{8,72},{9,... | collective-permute-start | bytes 516104 | tf_op jit(solution)/shard_map/ppermute | solution.py:42
  102.2 8.4 %collective-permute-start.19 = (bf16[96,896]{1,0:T(8,128)(2,1)S(1)}, bf16[96,896]{1,0:T(8,128)(2,1)S(1)}, u32[]{:S(2)}, u32[]{:S(2)}) collective-permute-start(bf16[96,896]{1,0:T(8,128)(2,1)S(1)} %get-tuple-element.90), channel_id=1, source_target_pairs={{0,32},{1,33},{2,34},{3,35},{4,36},{5,37},{6,38},{7,39},{8,40},{9,... | collective-permute-start | bytes 516104 | tf_op jit(solution)/shard_map/ppermute | solution.py:42
  103.0 8.5 %collective-permute-start.20 = (bf16[96,896]{1,0:T(8,128)(2,1)S(1)}, bf16[96,896]{1,0:T(8,128)(2,1)S(1)}, u32[]{:S(2)}, u32[]{:S(2)}) collective-permute-start(bf16[96,896]{1,0:T(8,128)(2,1)S(1)} %get-tuple-element.91), channel_id=1, source_target_pairs={{0,96},{1,97},{2,98},{3,99},{4,100},{5,101},{6,102},{7,103},{8,104... | collective-permute-start | bytes 516104 | tf_op jit(solution)/shard_map/ppermute | solution.py:42
where the time goes:
time: 113 us
  starting transfers between devices  36.2 us (32%)
  Pallas kernels  35.1 us (31%)
  waiting for transfers between devices  21 us (19%)
  blocking collectives  17.5 us (15%)
  local copies, waits for them, and re-layouts  2.65 us (2%)
    ppermute x21, starting transfers between devices, send(): return lax.ppermute(value, AXES, pairs)  36.2 us
    pallas_call x5, Pallas kernels, net(): pl.pallas_call(functools.partial(net_kernel, len(xs), tuple((p[1:] for p...  24.8 us
    ppermute x21, waiting for transfers between devices, send(): return lax.ppermute(value, AXES, pairs)  21 us
    all_to_all x1, blocking collectives, per_device(): lax.all_to_all(rows, 'expert', split_axis=0, concat_axis=0, tiled=True)  17.5 us
    pallas_call x3, Pallas kernels, last_net(): pl.pallas_call(functools.partial(last_kernel, tuple((t for _, t in pieces...  4.4 us
    pallas_call x2, Pallas kernels, pack(): pl.pallas_call(functools.partial(pack_kernel, len(rest)), out_shape=[pltp...  2.7 us
    unnamed x16, local copies, waits for them, and re-layouts  2.59 us
  transfers between devices with their start and end apart: 21, of which 13 were waited for; matrix products, arithmetic and copies ran while one was open for 0% of the time, Pallas kernels for 26%

commit v1 on v0

--- a/solution.py
+++ b/solution.py
@@ -284,7 +284,7 @@
             up = lax.dot_general(rows_in, gate_up[low + depth : low + 2 * depth], turned, preferred_element_type=F32)
             hidden = (gate / (1.0 + jnp.exp(-gate)) * up).astype(BF16)
             term = jnp.dot(hidden, down[starts[c] : starts[c] + depth], preferred_element_type=F32)
-            within = pl.ds(pl.multiple_of(sum_at + r * tile, tile), tile)
+            within = pl.ds(pl.multiple_of(sum_at + r * tile, EXPERTS * CAP), tile)
             if not outs and (add or c > 0):
                 sum_ref[within, :] += term
             elif not outs:

time: 113 us -> 113 us (level)
  no operation moved by 1% of the time
where the time goes in v1:
time: 113 us
  starting transfers between devices  36.2 us (32%)
  Pallas kernels  35.1 us (31%)
  waiting for transfers between devices  21 us (19%)
  blocking collectives  17.5 us (15%)
  local copies, waits for them, and re-layouts  2.65 us (2%)
    ppermute x21, starting transfers between devices, send(): return lax.ppermute(value, AXES, pairs)  36.2 us
    pallas_call x5, Pallas kernels, net(): pl.pallas_call(functools.partial(net_kernel, len(xs), tuple((p[1:] for p...  24.8 us
    ppermute x21, waiting for transfers between devices, send(): return lax.ppermute(value, AXES, pairs)  21 us
    all_to_all x1, blocking collectives, per_device(): lax.all_to_all(rows, 'expert', split_axis=0, concat_axis=0, tiled=True)  17.5 us
    pallas_call x3, Pallas kernels, last_net(): pl.pallas_call(functools.partial(last_kernel, tuple((t for _, t in pieces...  4.4 us
    pallas_call x2, Pallas kernels, pack(): pl.pallas_call(functools.partial(pack_kernel, len(rest)), out_shape=[pltp...  2.7 us
    unnamed x16, local copies, waits for them, and re-layouts  2.59 us
  transfers between devices with their start and end apart: 21, of which 13 were waited for; matrix products, arithmetic and copies ran while one was open for 0% of the time, Pallas kernels for 26%

profile of v1, /device:TPU:1, one launch (start us, length us, event | category | flops | bytes accessed | tf_op | source)
XLA Modules:
  0.0 112.7 jit_solution(12673564296881427380)
XLA Ops:
  0.0 2.5 %pack_weights.2 = (bf16[912,896]{1,0:T(8,128)(2,1)S(1)}, bf16[384,896]{1,0:T(8,128)(2,1)S(1)}) custom-call(bf16[304,896]{1,0:T(8,128)(2,1)} %bitcast.32, bf16[304,896]{1,0:T(8,128)(2,1)} %bitcast.33, bf16[304,896]{1,0:T(8,128)(2,1)} %bitcast.34, s32[2,128]{1,0:T(2,128)} %bitcast.29, bf16[128,896]{1,0:T(8,128)(2,1)} %refs_4_.1), custom_call_target="tpu_custom_call" | custom-call | flops 100000000 | bytes 4000000 | tf_op jit(solution)/shard_map/pack_weights/pallas_call | solution.py:98
  2.5 2.2 %collective-permute-start = (bf16[912,896]{1,0:T(8,128)(2,1)S(1)}, bf16[912,896]{1,0:T(8,128)(2,1)S(1)}, u32[]{:S(2)}, u32[]{:S(2)}) collective-permute-start(bf16[912,896]{1,0:T(8,128)(2,1)S(1)} %get-tuple-element.56.refs_1_.refs_0_.refs_2_), channel_id=1, source_target_pairs={{0,1},{1,2},{2,3},{3,0},{4,5},{5,6},{6,7},{7,4},{8,9},{9,10},{10,1... | collective-permute-start | bytes 4902920 | tf_op jit(solution)/shard_map/ppermute | solution.py:42
  4.7 0.0 copy-done.4
  4.7 0.2 pack_weights.3.refs_2_.refs_1_.refs_3_
  4.9 1.5 %collective-permute-start.1 = (bf16[912,896]{1,0:T(8,128)(2,1)S(1)}, bf16[912,896]{1,0:T(8,128)(2,1)S(1)}, u32[]{:S(2)}, u32[]{:S(2)}) collective-permute-start(bf16[912,896]{1,0:T(8,128)(2,1)S(1)} %pack_weights.3.refs_2_.refs_1_.refs_3_), channel_id=1, source_target_pairs={{0,3},{1,0},{2,1},{3,2},{4,7},{5,4},{6,5},{7,6},{8,11},{9,8},{10,9... | collective-permute-start | bytes 4902920 | tf_op jit(solution)/shard_map/ppermute | solution.py:42
  6.5 17.5 %all_to_all.5 = bf16[8,48,896]{2,1,0:T(8,128)(2,1)S(1)} all-to-all(bf16[8,48,896]{2,1,0:T(8,128)(2,1)S(1)} %bitcast.25), channel_id=1, replica_groups=mesh['expert'=8,'shard'=16] {'expert'}, dimensions={0} | all-to-all | bytes 1376256 | tf_op jit(solution)/shard_map/all_to_all | solution.py:391
  24.0 0.2 collective-permute-start.2
  24.1 2.5 %collective-permute-start.3 = (bf16[384,896]{1,0:T(8,128)(2,1)S(1)}, bf16[384,896]{1,0:T(8,128)(2,1)S(1)}, u32[]{:S(2)}, u32[]{:S(2)}) collective-permute-start(bf16[384,896]{1,0:T(8,128)(2,1)S(1)} %bitcast.20), channel_id=1, source_target_pairs={{0,12},{1,13},{2,14},{3,15},{4,0},{5,1},{6,2},{7,3},{8,4},{9,5},{1... | collective-permute-start | bytes 2064392 | tf_op jit(solution)/shard_map/ppermute | solution.py:42
  26.6 0.0 collective-permute-done.refs_3_.refs_4_
  26.6 0.0 collective-permute-done.1.refs_4_.refs_5_
  26.6 3.4 %networks.5.refs_6_ = f32[1536,896]{1,0:T(8,128)S(1)} custom-call(bf16[384,896]{1,0:T(8,128)(2,1)S(1)} %bitcast.21, bf16[912,896]{1,0:T(8,128)(2,1)S(1)} %get-tuple-element.56.refs_1_.refs_0_.refs_2_, bf16[912,896]{1,0:T(8,128)(2,1)S(1)} %pack_weights.3.refs_2_.refs_1_.refs_3_, bf16[912,896]{1,0:T(8,128)(2,1)S(1)} %collective-permute-done.refs_3_.refs_4_, ...), custom_call_target="tpu_custom_call" | custom-call | flops 2642411520 | bytes 9633792 | tf_op jit(solution)/shard_map/networks/pallas_call | solution.py:356
  30.1 1.4 %collective-permute-start.6 = (bf16[912,896]{1,0:T(8,128)(2,1)S(1)}, bf16[912,896]{1,0:T(8,128)(2,1)S(1)}, u32[]{:S(2)}, u32[]{:S(2)}) collective-permute-start(bf16[912,896]{1,0:T(8,128)(2,1)S(1)} %collective-permute-done.refs_3_.refs_4_), channel_id=1, source_target_pairs={{0,1},{1,2},{2,3},{3,0},{4,5},{5,6},{6,7},{7,4},{8,9},{9,10},{10,1... | collective-permute-start | bytes 4902920 | tf_op jit(solution)/shard_map/ppermute | solution.py:42
  31.4 1.5 %collective-permute-start.7 = (bf16[912,896]{1,0:T(8,128)(2,1)S(1)}, bf16[912,896]{1,0:T(8,128)(2,1)S(1)}, u32[]{:S(2)}, u32[]{:S(2)}) collective-permute-start(bf16[912,896]{1,0:T(8,128)(2,1)S(1)} %collective-permute-done.1.refs_4_.refs_5_), channel_id=1, source_target_pairs={{0,3},{1,0},{2,1},{3,2},{4,7},{5,4},{6,5},{7,6},{8,11},{9,8},{10,9... | collective-permute-start | bytes 4902920 | tf_op jit(solution)/shard_map/ppermute | solution.py:42
  32.9 0.2 split_weights.1
  33.2 2.1 %collective-permute-done.2.refs_1_.refs_3_.refs_2_ = bf16[384,896]{1,0:T(8,128)(2,1)S(1)} collective-permute-done((bf16[384,896]{1,0:T(8,128)(2,1)S(1)}, bf16[384,896]{1,0:T(8,128)(2,1)S(1)}, u32[]{:S(2)}, u32[]{:S(2)}) %collective-permute-start.2) | collective-permute-done | bytes 688160 | tf_op jit(solution)/shard_map/ppermute | solution.py:42
  35.2 0.0 collective-permute-done.3.refs_0_.refs_2_.refs_1_
  35.3 0.3 collective-permute-start.4
  35.6 2.6 %collective-permute-start.5 = (bf16[192,896]{1,0:T(8,128)(2,1)S(1)}, bf16[192,896]{1,0:T(8,128)(2,1)S(1)}, u32[]{:S(2)}, u32[]{:S(2)}) collective-permute-start(bf16[192,896]{1,0:T(8,128)(2,1)S(1)} %slice.7), channel_id=1, source_target_pairs={{0,12},{1,13},{2,14},{3,15},{4,0},{5,1},{6,2},{7,3},{8,4},{9,5},{1... | collective-permute-start | bytes 1032200 | tf_op jit(solution)/shard_map/ppermute | solution.py:42
  38.1 6.5 %networks.6.refs_6_ = f32[1536,896]{1,0:T(8,128)S(1)} custom-call(bf16[384,896]{1,0:T(8,128)(2,1)S(1)} %collective-permute-done.3.refs_0_.refs_2_.refs_1_, bf16[384,896]{1,0:T(8,128)(2,1)S(1)} %collective-permute-done.2.refs_1_.refs_3_.refs_2_, bf16[912,896]{1,0:T(8,128)(2,1)S(1)} %get-tuple-element.56.refs_1_.refs_0_.refs_2_, ...), custom_call_target="tpu_custom_call", output_to_operand_aliasing={{}: (6, {})} | custom-call | flops 5284823040 | bytes 12386304 | tf_op jit(solution)/shard_map/networks/pallas_call | solution.py:356
  44.7 1.9 %collective-permute-start.10 = (bf16[528,896]{1,0:T(8,128)(2,1)S(1)}, bf16[528,896]{1,0:T(8,128)(2,1)S(1)}, u32[]{:S(2)}, u32[]{:S(2)}) collective-permute-start(bf16[528,896]{1,0:T(8,128)(2,1)S(1)} %get-tuple-element.76), channel_id=1, source_target_pairs={{0,1},{1,2},{2,3},{3,0},{4,5},{5,6},{6,7},{7,4},{8,9},{9,10},{10,1... | collective-permute-start | bytes 2838536 | tf_op jit(solution)/shard_map/ppermute | solution.py:42
  46.6 0.1 collective-permute-done.4.refs_0_
  46.7 3.1 %collective-permute-start.11 = (bf16[528,896]{1,0:T(8,128)(2,1)S(1)}, bf16[528,896]{1,0:T(8,128)(2,1)S(1)}, u32[]{:S(2)}, u32[]{:S(2)}) collective-permute-start(bf16[528,896]{1,0:T(8,128)(2,1)S(1)} %get-tuple-element.77), channel_id=1, source_target_pairs={{0,3},{1,0},{2,1},{3,2},{4,7},{5,4},{6,5},{7,6},{8,11},{9,8},{10,9... | collective-permute-start | bytes 2838536 | tf_op jit(solution)/shard_map/ppermute | solution.py:42
  49.8 0.0 collective-permute-done.5.refs_1_
  49.8 3.4 %networks.7.refs_7_ = f32[1536,896]{1,0:T(8,128)S(1)} custom-call(bf16[192,896]{1,0:T(8,128)(2,1)S(1)} %collective-permute-done.4.refs_0_, bf16[192,896]{1,0:T(8,128)(2,1)S(1)} %collective-permute-done.5.refs_1_, bf16[912,896]{1,0:T(8,128)(2,1)S(1)} %get-tuple-element.56.refs_1_.refs_0_.refs_2_, ...), custom_call_target="tpu_custom_call", output_to_operand_aliasing={{}: (6, {})} | custom-call | flops 2642411520 | bytes 9633792 | tf_op jit(solution)/shard_map/networks/pallas_call | solution.py:356
  53.2 4.6 %collective-permute-done.6.refs_5_ = bf16[912,896]{1,0:T(8,128)(2,1)S(1)} collective-permute-done((bf16[912,896]{1,0:T(8,128)(2,1)S(1)}, bf16[912,896]{1,0:T(8,128)(2,1)S(1)}, u32[]{:S(2)}, u32[]{:S(2)}) %collective-permute-start.6) | collective-permute-done | bytes 1634336 | tf_op jit(solution)/shard_map/ppermute | solution.py:42
  57.8 0.4 collective-permute-done.7.refs_6_.refs_5_
  58.2 1.3 %collective-permute-start.8 = (bf16[384,896]{1,0:T(8,128)(2,1)S(1)}, bf16[384,896]{1,0:T(8,128)(2,1)S(1)}, u32[]{:S(2)}, u32[]{:S(2)}) collective-permute-start(bf16[384,896]{1,0:T(8,128)(2,1)S(1)} %get-tuple-element.73), channel_id=1, source_target_pairs={{0,1},{1,2},{2,3},{3,0},{4,5},{5,6},{6,7},{7,4},{8,9},{9,10},{10,1... | collective-permute-start | bytes 2064392 | tf_op jit(solution)/shard_map/ppermute | solution.py:42
  59.5 1.4 %collective-permute-start.9 = (bf16[384,896]{1,0:T(8,128)(2,1)S(1)}, bf16[384,896]{1,0:T(8,128)(2,1)S(1)}, u32[]{:S(2)}, u32[]{:S(2)}) collective-permute-start(bf16[384,896]{1,0:T(8,128)(2,1)S(1)} %get-tuple-element.74), channel_id=1, source_target_pairs={{0,3},{1,0},{2,1},{3,2},{4,7},{5,4},{6,5},{7,6},{8,11},{9,8},{10,9... | collective-permute-start | bytes 2064392 | tf_op jit(solution)/shard_map/ppermute | solution.py:42
  60.9 5.7 %networks.8.refs_8_ = f32[1536,896]{1,0:T(8,128)S(1)} custom-call(bf16[192,896]{1,0:T(8,128)(2,1)S(1)} %collective-permute-done.4.refs_0_, bf16[192,896]{1,0:T(8,128)(2,1)S(1)} %collective-permute-done.5.refs_1_, bf16[384,896]{1,0:T(8,128)(2,1)S(1)} %collective-permute-done.3.refs_0_.refs_2_.refs_1_, ...), custom_call_target="tpu_custom_call", output_to_operand_aliasing={{}: (7, {})} | custom-call | flops 4227858432 | bytes 13762560 | tf_op jit(solution)/shard_map/networks/pallas_call | solution.py:356
  66.6 1.4 %collective-permute-done.10.refs_6_ = bf16[528,896]{1,0:T(8,128)(2,1)S(1)} collective-permute-done((bf16[528,896]{1,0:T(8,128)(2,1)S(1)}, bf16[528,896]{1,0:T(8,128)(2,1)S(1)}, u32[]{:S(2)}, u32[]{:S(2)}) %collective-permute-start.10) | collective-permute-done | bytes 946208 | tf_op jit(solution)/shard_map/ppermute | solution.py:42
  68.0 0.4 collective-permute-done.11.refs_7_
  68.3 5.7 %networks.9.refs_4_.refs_5_.refs_3_ = f32[1536,896]{1,0:T(8,128)S(1)} custom-call(bf16[192,896]{1,0:T(8,128)(2,1)S(1)} %collective-permute-done.4.refs_0_, bf16[192,896]{1,0:T(8,128)(2,1)S(1)} %collective-permute-done.5.refs_1_, bf16[384,896]{1,0:T(8,128)(2,1)S(1)} %collective-permute-done.3.refs_0_.refs_2_.refs_1_, ...), custom_call_target="tpu_custom_call", output_to_operand_aliasing={{}: (8, {})} | custom-call | flops 4227858432 | bytes 13762560 | tf_op jit(solution)/shard_map/networks/pallas_call | solution.py:356
  74.1 0.0 copy-start
  74.1 1.0 collective-permute-done.8.refs_2_.refs_3_.refs_1_
  75.0 0.4 collective-permute-done.9.refs_3_.refs_4_.refs_2_
  75.4 1.7 %networks_last.3 = bf16[384,896]{1,0:T(8,128)(2,1)} custom-call(bf16[192,896]{1,0:T(8,128)(2,1)S(1)} %collective-permute-done.4.refs_0_, bf16[192,896]{1,0:T(8,128)(2,1)S(1)} %collective-permute-done.5.refs_1_, bf16[384,896]{1,0:T(8,128)(2,1)S(1)} %collective-permute-done.8.refs_2_.refs_3_.refs_1_, ...), custom_call_target="tpu_custom_call" | custom-call | flops 528482304 | bytes 4128768 | tf_op jit(solution)/shard_map/networks_last/pallas_call | solution.py:335
  77.1 1.5 %collective-permute-start.12 = (bf16[384,896]{1,0:T(8,128)(2,1)}, bf16[384,896]{1,0:T(8,128)(2,1)}, u32[]{:S(2)}, u32[]{:S(2)}) collective-permute-start(bf16[384,896]{1,0:T(8,128)(2,1)} %networks_last.3), channel_id=1, source_target_pairs={{0,8},{1,9},{2,10},{3,11},{4,12},{5,13},{6,14},{7,15},{8,0},{9,1},... | collective-permute-start | bytes 2064392 | tf_op jit(solution)/shard_map/ppermute | solution.py:42
  78.7 2.6 %copy-done.1 = f32[1536,896]{1,0:T(8,128)S(1)} copy-done((f32[1536,896]{1,0:T(8,128)S(1)}, f32[1536,896]{1,0:T(8,128)}, u32[]{:S(2)}) %copy-start.1) | copy-done | bytes 5505048
  81.2 1.8 %networks_last.4 = (bf16[192,896]{1,0:T(8,128)(2,1)S(1)}, bf16[192,896]{1,0:T(8,128)(2,1)S(1)}, bf16[192,896]{1,0:T(8,128)(2,1)S(1)}, bf16[192,896]{1,0:T(8,128)(2,1)S(1)}) custom-call(s32[1]{0:T(128)} %bitcast.refs_0_.here_ref, bf16[384,896]{1,0:T(8,128)(2,1)S(1)} %collective-permute-done.3.refs_0_.refs_2_.refs_1_, ...), custom_call_target="tpu_custom_call" | custom-call | flops 1056964608 | bytes 6881280 | tf_op jit(solution)/shard_map/networks_last/pallas_call | solution.py:335
  83.0 0.7 collective-permute-start.13
  83.7 2.1 %collective-permute-start.14 = (bf16[192,896]{1,0:T(8,128)(2,1)S(1)}, bf16[192,896]{1,0:T(8,128)(2,1)S(1)}, u32[]{:S(2)}, u32[]{:S(2)}) collective-permute-start(bf16[192,896]{1,0:T(8,128)(2,1)S(1)} %get-tuple-element.85), channel_id=1, source_target_pairs={{0,12},{1,13},{2,14},{3,15},{4,0},{5,1},{6,2},{7,3},{8,4},{9,5},{1... | collective-permute-start | bytes 1032200 | tf_op jit(solution)/shard_map/ppermute | solution.py:42
  85.8 1.8 %collective-permute-start.16 = (bf16[192,896]{1,0:T(8,128)(2,1)S(1)}, bf16[192,896]{1,0:T(8,128)(2,1)S(1)}, u32[]{:S(2)}, u32[]{:S(2)}) collective-permute-start(bf16[192,896]{1,0:T(8,128)(2,1)S(1)} %get-tuple-element.87), channel_id=1, source_target_pairs={{0,20},{1,21},{2,22},{3,23},{4,24},{5,25},{6,26},{7,27},{8,28},{9,... | collective-permute-start | bytes 1032200 | tf_op jit(solution)/shard_map/ppermute | solution.py:42
  87.6 1.9 %collective-permute-start.17 = (bf16[192,896]{1,0:T(8,128)(2,1)S(1)}, bf16[192,896]{1,0:T(8,128)(2,1)S(1)}, u32[]{:S(2)}, u32[]{:S(2)}) collective-permute-start(bf16[192,896]{1,0:T(8,128)(2,1)S(1)} %get-tuple-element.88), channel_id=1, source_target_pairs={{0,28},{1,29},{2,30},{3,31},{4,16},{5,17},{6,18},{7,19},{8,20},{9,... | collective-permute-start | bytes 1032200 | tf_op jit(solution)/shard_map/ppermute | solution.py:42
  89.5 0.9 networks_last.5.own_ref
  90.4 0.0 collective-permute-done.12.far_ref
  90.4 1.2 %halve_rows.1 = (f32[192,896]{1,0:T(8,128)S(1)}, bf16[192,896]{1,0:T(8,128)(2,1)S(1)}) custom-call(s32[1]{0:T(128)} %bitcast.refs_0_.here_ref, f32[384,896]{1,0:T(8,128)S(1)} %networks_last.5.own_ref, bf16[384,896]{1,0:T(8,128)(2,1)} %collective-permute-done.12.far_ref), custom_call_target="tpu_custom_call" | custom-call | flops 1000000 | bytes 3000000 | tf_op jit(solution)/shard_map/halve_rows/pallas_call | solution.py:173
  91.7 0.0 copy-start.6
  91.7 0.0 copy-start.7
  91.7 0.1 collective-permute-start.15
  91.8 0.9 collective-permute-done.13.prev_ref
  92.6 0.0 collective-permute-done.14.next_ref
  92.6 3.7 %collective-permute-done.16.prev_other_ref = bf16[192,896]{1,0:T(8,128)(2,1)S(1)} collective-permute-done((bf16[192,896]{1,0:T(8,128)(2,1)S(1)}, bf16[192,896]{1,0:T(8,128)(2,1)S(1)}, u32[]{:S(2)}, u32[]{:S(2)}) %collective-permute-start.16) | collective-permute-done | bytes 344096 | tf_op jit(solution)/shard_map/ppermute | solution.py:42
  96.3 0.0 collective-permute-done.17.next_other_ref
  96.3 0.0 collective-permute-done.15.given_ref
  96.3 0.2 sum_rows.1
  96.6 5.6 %collective-permute-start.18 = (bf16[96,896]{1,0:T(8,128)(2,1)S(1)}, bf16[96,896]{1,0:T(8,128)(2,1)S(1)}, u32[]{:S(2)}, u32[]{:S(2)}) collective-permute-start(bf16[96,896]{1,0:T(8,128)(2,1)S(1)} %get-tuple-element.89), channel_id=1, source_target_pairs={{0,64},{1,65},{2,66},{3,67},{4,68},{5,69},{6,70},{7,71},{8,72},{9,... | collective-permute-start | bytes 516104 | tf_op jit(solution)/shard_map/ppermute | solution.py:42
  102.2 0.7 collective-permute-start.19
  103.0 1.9 %collective-permute-start.20 = (bf16[96,896]{1,0:T(8,128)(2,1)S(1)}, bf16[96,896]{1,0:T(8,128)(2,1)S(1)}, u32[]{:S(2)}, u32[]{:S(2)}) collective-permute-start(bf16[96,896]{1,0:T(8,128)(2,1)S(1)} %get-tuple-element.91), channel_id=1, source_target_pairs={{0,96},{1,97},{2,98},{3,99},{4,100},{5,101},{6,102},{7,103},{8,104... | collective-permute-start | bytes 516104 | tf_op jit(solution)/shard_map/ppermute | solution.py:42
  104.9 0.0 copy-done.7
  104.9 0.3 gate_shares.1
  105.2 1.7 %collective-permute-done.18.refs_0_ = bf16[96,896]{1,0:T(8,128)(2,1)S(1)} collective-permute-done((bf16[96,896]{1,0:T(8,128)(2,1)S(1)}, bf16[96,896]{1,0:T(8,128)(2,1)S(1)}, u32[]{:S(2)}, u32[]{:S(2)}) %collective-permute-start.18) | collective-permute-done | bytes 172064 | tf_op jit(solution)/shard_map/ppermute | solution.py:42
  106.9 3.8 %collective-permute-done.19.refs_1_ = bf16[96,896]{1,0:T(8,128)(2,1)S(1)} collective-permute-done((bf16[96,896]{1,0:T(8,128)(2,1)S(1)}, bf16[96,896]{1,0:T(8,128)(2,1)S(1)}, u32[]{:S(2)}, u32[]{:S(2)}) %collective-permute-start.19) | collective-permute-done | bytes 172064 | tf_op jit(solution)/shard_map/ppermute | solution.py:42
  110.7 0.8 collective-permute-done.20.refs_2_
  111.4 1.2 %combine_rows.1 = bf16[128,896]{1,0:T(8,128)(2,1)} custom-call(s32[1]{0:T(128)} %bitcast.refs_0_.here_ref, bf16[128,384]{1,0:T(8,128)(2,1)S(1)} %get-tuple-element.49.high_ref, bf16[128,384]{1,0:T(8,128)(2,1)S(1)} %get-tuple-element.50.low_ref, bf16[96,896]{1,0:T(8,128)(2,1)S(1)} %collective-permute-done.18.refs_0_, ...), custom_call_target="tpu_custom_call" | custom-call | flops 200000000 | bytes 1000000 | tf_op jit(solution)/shard_map/combine_rows/pallas_call | solution.py:222
  (12 shorter events, 0.1 us)
Async XLA Ops:
  0.0 4.7 %copy-start.4 = (bf16[1,896,304]{1,2,0:T(8,128)(2,1)S(1)}, bf16[1,896,304]{1,2,0:T(8,128)(2,1)}, u32[]{:S(2)}) copy-start(bf16[1,896,304]{1,2,0:T(8,128)(2,1)} %param.16) | copy-start | bytes 1634308
  0.0 4.7 %copy-start.5 = (bf16[1,304,896]{2,1,0:T(8,128)(2,1)S(1)}, bf16[1,304,896]{2,1,0:T(8,128)(2,1)}, u32[]{:S(2)}) copy-start(bf16[1,304,896]{2,1,0:T(8,128)(2,1)} %param.17) | copy-start | bytes 1634308
  0.0 4.7 %copy-start.3 = (bf16[1,896,304]{1,2,0:T(8,128)(2,1)S(1)}, bf16[1,896,304]{1,2,0:T(8,128)(2,1)}, u32[]{:S(2)}) copy-start(bf16[1,896,304]{1,2,0:T(8,128)(2,1)} %param.15) | copy-start | bytes 1634308
  2.5 24.1 %collective-permute-start = (bf16[912,896]{1,0:T(8,128)(2,1)S(1)}, bf16[912,896]{1,0:T(8,128)(2,1)S(1)}, u32[]{:S(2)}, u32[]{:S(2)}) collective-permute-start(bf16[912,896]{1,0:T(8,128)(2,1)S(1)} %get-tuple-element.56.refs_1_.refs_0_.refs_2_), channel_id=1, source_target_pairs={{0,1},{1,2},{2,3},{3,0},{4,5},{5,6},{6,7},{7,4},{8,9},{9,10},{10,1... | collective-permute-start | bytes 4902920 | tf_op jit(solution)/shard_map/ppermute | solution.py:42
  4.9 21.7 %collective-permute-start.1 = (bf16[912,896]{1,0:T(8,128)(2,1)S(1)}, bf16[912,896]{1,0:T(8,128)(2,1)S(1)}, u32[]{:S(2)}, u32[]{:S(2)}) collective-permute-start(bf16[912,896]{1,0:T(8,128)(2,1)S(1)} %pack_weights.3.refs_2_.refs_1_.refs_3_), channel_id=1, source_target_pairs={{0,3},{1,0},{2,1},{3,2},{4,7},{5,4},{6,5},{7,6},{8,11},{9,8},{10,9... | collective-permute-start | bytes 4902920 | tf_op jit(solution)/shard_map/ppermute | solution.py:42
  24.0 11.3 %collective-permute-start.2 = (bf16[384,896]{1,0:T(8,128)(2,1)S(1)}, bf16[384,896]{1,0:T(8,128)(2,1)S(1)}, u32[]{:S(2)}, u32[]{:S(2)}) collective-permute-start(bf16[384,896]{1,0:T(8,128)(2,1)S(1)} %bitcast.19), channel_id=1, source_target_pairs={{0,4},{1,5},{2,6},{3,7},{4,8},{5,9},{6,10},{7,11},{8,12},{9,13},{1... | collective-permute-start | bytes 2064392 | tf_op jit(solution)/shard_map/ppermute | solution.py:42
  24.1 11.1 %collective-permute-start.3 = (bf16[384,896]{1,0:T(8,128)(2,1)S(1)}, bf16[384,896]{1,0:T(8,128)(2,1)S(1)}, u32[]{:S(2)}, u32[]{:S(2)}) collective-permute-start(bf16[384,896]{1,0:T(8,128)(2,1)S(1)} %bitcast.20), channel_id=1, source_target_pairs={{0,12},{1,13},{2,14},{3,15},{4,0},{5,1},{6,2},{7,3},{8,4},{9,5},{1... | collective-permute-start | bytes 2064392 | tf_op jit(solution)/shard_map/ppermute | solution.py:42
  30.1 27.8 %collective-permute-start.6 = (bf16[912,896]{1,0:T(8,128)(2,1)S(1)}, bf16[912,896]{1,0:T(8,128)(2,1)S(1)}, u32[]{:S(2)}, u32[]{:S(2)}) collective-permute-start(bf16[912,896]{1,0:T(8,128)(2,1)S(1)} %collective-permute-done.refs_3_.refs_4_), channel_id=1, source_target_pairs={{0,1},{1,2},{2,3},{3,0},{4,5},{5,6},{6,7},{7,4},{8,9},{9,10},{10,1... | collective-permute-start | bytes 4902920 | tf_op jit(solution)/shard_map/ppermute | solution.py:42
  31.4 26.8 %collective-permute-start.7 = (bf16[912,896]{1,0:T(8,128)(2,1)S(1)}, bf16[912,896]{1,0:T(8,128)(2,1)S(1)}, u32[]{:S(2)}, u32[]{:S(2)}) collective-permute-start(bf16[912,896]{1,0:T(8,128)(2,1)S(1)} %collective-permute-done.1.refs_4_.refs_5_), channel_id=1, source_target_pairs={{0,3},{1,0},{2,1},{3,2},{4,7},{5,4},{6,5},{7,6},{8,11},{9,8},{10,9... | collective-permute-start | bytes 4902920 | tf_op jit(solution)/shard_map/ppermute | solution.py:42
  35.3 11.4 %collective-permute-start.4 = (bf16[192,896]{1,0:T(8,128)(2,1)S(1)}, bf16[192,896]{1,0:T(8,128)(2,1)S(1)}, u32[]{:S(2)}, u32[]{:S(2)}) collective-permute-start(bf16[192,896]{1,0:T(8,128)(2,1)S(1)} %slice.6), channel_id=1, source_target_pairs={{0,4},{1,5},{2,6},{3,7},{4,8},{5,9},{6,10},{7,11},{8,12},{9,13},{1... | collective-permute-start | bytes 1032200 | tf_op jit(solution)/shard_map/ppermute | solution.py:42
  35.6 14.2 %collective-permute-start.5 = (bf16[192,896]{1,0:T(8,128)(2,1)S(1)}, bf16[192,896]{1,0:T(8,128)(2,1)S(1)}, u32[]{:S(2)}, u32[]{:S(2)}) collective-permute-start(bf16[192,896]{1,0:T(8,128)(2,1)S(1)} %slice.7), channel_id=1, source_target_pairs={{0,12},{1,13},{2,14},{3,15},{4,0},{5,1},{6,2},{7,3},{8,4},{9,5},{1... | collective-permute-start | bytes 1032200 | tf_op jit(solution)/shard_map/ppermute | solution.py:42
  44.7 23.3 %collective-permute-start.10 = (bf16[528,896]{1,0:T(8,128)(2,1)S(1)}, bf16[528,896]{1,0:T(8,128)(2,1)S(1)}, u32[]{:S(2)}, u32[]{:S(2)}) collective-permute-start(bf16[528,896]{1,0:T(8,128)(2,1)S(1)} %get-tuple-element.76), channel_id=1, source_target_pairs={{0,1},{1,2},{2,3},{3,0},{4,5},{5,6},{6,7},{7,4},{8,9},{9,10},{10,1... | collective-permute-start | bytes 2838536 | tf_op jit(solution)/shard_map/ppermute | solution.py:42
  46.7 21.6 %collective-permute-start.11 = (bf16[528,896]{1,0:T(8,128)(2,1)S(1)}, bf16[528,896]{1,0:T(8,128)(2,1)S(1)}, u32[]{:S(2)}, u32[]{:S(2)}) collective-permute-start(bf16[528,896]{1,0:T(8,128)(2,1)S(1)} %get-tuple-element.77), channel_id=1, source_target_pairs={{0,3},{1,0},{2,1},{3,2},{4,7},{5,4},{6,5},{7,6},{8,11},{9,8},{10,9... | collective-permute-start | bytes 2838536 | tf_op jit(solution)/shard_map/ppermute | solution.py:42
  58.2 16.9 %collective-permute-start.8 = (bf16[384,896]{1,0:T(8,128)(2,1)S(1)}, bf16[384,896]{1,0:T(8,128)(2,1)S(1)}, u32[]{:S(2)}, u32[]{:S(2)}) collective-permute-start(bf16[384,896]{1,0:T(8,128)(2,1)S(1)} %get-tuple-element.73), channel_id=1, source_target_pairs={{0,1},{1,2},{2,3},{3,0},{4,5},{5,6},{6,7},{7,4},{8,9},{9,10},{10,1... | collective-permute-start | bytes 2064392 | tf_op jit(solution)/shard_map/ppermute | solution.py:42
  59.5 15.9 %collective-permute-start.9 = (bf16[384,896]{1,0:T(8,128)(2,1)S(1)}, bf16[384,896]{1,0:T(8,128)(2,1)S(1)}, u32[]{:S(2)}, u32[]{:S(2)}) collective-permute-start(bf16[384,896]{1,0:T(8,128)(2,1)S(1)} %get-tuple-element.74), channel_id=1, source_target_pairs={{0,3},{1,0},{2,1},{3,2},{4,7},{5,4},{6,5},{7,6},{8,11},{9,8},{10,9... | collective-permute-start | bytes 2064392 | tf_op jit(solution)/shard_map/ppermute | solution.py:42
  74.1 3.1 %copy-start = (f32[1536,896]{1,0:T(8,128)}, f32[1536,896]{1,0:T(8,128)S(1)}, u32[]{:S(2)}) copy-start(f32[1536,896]{1,0:T(8,128)S(1)} %networks.9.refs_4_.refs_5_.refs_3_) | copy-start | bytes 16515076
  77.1 13.3 %collective-permute-start.12 = (bf16[384,896]{1,0:T(8,128)(2,1)}, bf16[384,896]{1,0:T(8,128)(2,1)}, u32[]{:S(2)}, u32[]{:S(2)}) collective-permute-start(bf16[384,896]{1,0:T(8,128)(2,1)} %networks_last.3), channel_id=1, source_target_pairs={{0,8},{1,9},{2,10},{3,11},{4,12},{5,13},{6,14},{7,15},{8,0},{9,1},... | collective-permute-start | bytes 2064392 | tf_op jit(solution)/shard_map/ppermute | solution.py:42
  78.7 2.6 %copy-start.1 = (f32[1536,896]{1,0:T(8,128)S(1)}, f32[1536,896]{1,0:T(8,128)}, u32[]{:S(2)}) copy-start(f32[1536,896]{1,0:T(8,128)} %copy-done) | copy-start | bytes 16515076
  81.2 8.3 %copy-start.2 = (f32[1536,896]{1,0:T(8,128)S(1)}, f32[1536,896]{1,0:T(8,128)}, u32[]{:S(2)}) copy-start(f32[1536,896]{1,0:T(8,128)} %copy-done) | copy-start | bytes 16515076
  83.0 9.6 %collective-permute-start.13 = (bf16[192,896]{1,0:T(8,128)(2,1)S(1)}, bf16[192,896]{1,0:T(8,128)(2,1)S(1)}, u32[]{:S(2)}, u32[]{:S(2)}) collective-permute-start(bf16[192,896]{1,0:T(8,128)(2,1)S(1)} %get-tuple-element.81), channel_id=1, source_target_pairs={{0,4},{1,5},{2,6},{3,7},{4,8},{5,9},{6,10},{7,11},{8,12},{9,13},{1... | collective-permute-start | bytes 1032200 | tf_op jit(solution)/shard_map/ppermute | solution.py:42
  83.7 8.9 %collective-permute-start.14 = (bf16[192,896]{1,0:T(8,128)(2,1)S(1)}, bf16[192,896]{1,0:T(8,128)(2,1)S(1)}, u32[]{:S(2)}, u32[]{:S(2)}) collective-permute-start(bf16[192,896]{1,0:T(8,128)(2,1)S(1)} %get-tuple-element.85), channel_id=1, source_target_pairs={{0,12},{1,13},{2,14},{3,15},{4,0},{5,1},{6,2},{7,3},{8,4},{9,5},{1... | collective-permute-start | bytes 1032200 | tf_op jit(solution)/shard_map/ppermute | solution.py:42
  85.8 10.5 %collective-permute-start.16 = (bf16[192,896]{1,0:T(8,128)(2,1)S(1)}, bf16[192,896]{1,0:T(8,128)(2,1)S(1)}, u32[]{:S(2)}, u32[]{:S(2)}) collective-permute-start(bf16[192,896]{1,0:T(8,128)(2,1)S(1)} %get-tuple-element.87), channel_id=1, source_target_pairs={{0,20},{1,21},{2,22},{3,23},{4,24},{5,25},{6,26},{7,27},{8,28},{9,... | collective-permute-start | bytes 1032200 | tf_op jit(solution)/shard_map/ppermute | solution.py:42
  87.6 8.7 %collective-permute-start.17 = (bf16[192,896]{1,0:T(8,128)(2,1)S(1)}, bf16[192,896]{1,0:T(8,128)(2,1)S(1)}, u32[]{:S(2)}, u32[]{:S(2)}) collective-permute-start(bf16[192,896]{1,0:T(8,128)(2,1)S(1)} %get-tuple-element.88), channel_id=1, source_target_pairs={{0,28},{1,29},{2,30},{3,31},{4,16},{5,17},{6,18},{7,19},{8,20},{9,... | collective-permute-start | bytes 1032200 | tf_op jit(solution)/shard_map/ppermute | solution.py:42
  91.7 13.2 %copy-start.6 = (s32[128,2]{0,1:T(2,128)S(1)}, s32[128,2]{0,1:T(2,128)}, u32[]{:S(2)}) copy-start(s32[128,2]{0,1:T(2,128)} %param.10) | copy-start | bytes 3076
  91.7 13.2 %copy-start.7 = (s32[128,2]{0,1:T(2,128)S(1)}, s32[128,2]{0,1:T(2,128)}, u32[]{:S(2)}) copy-start(s32[128,2]{0,1:T(2,128)} %param.11) | copy-start | bytes 3076
  91.7 4.6 %collective-permute-start.15 = (bf16[192,896]{1,0:T(8,128)(2,1)S(1)}, bf16[192,896]{1,0:T(8,128)(2,1)S(1)}, u32[]{:S(2)}, u32[]{:S(2)}) collective-permute-start(bf16[192,896]{1,0:T(8,128)(2,1)S(1)} %get-tuple-element.86), channel_id=1, source_target_pairs={{0,16},{1,17},{2,18},{3,19},{4,20},{5,21},{6,22},{7,23},{8,24},{9,... | collective-permute-start | bytes 1032200 | tf_op jit(solution)/shard_map/ppermute | solution.py:42
  96.6 10.3 %collective-permute-start.18 = (bf16[96,896]{1,0:T(8,128)(2,1)S(1)}, bf16[96,896]{1,0:T(8,128)(2,1)S(1)}, u32[]{:S(2)}, u32[]{:S(2)}) collective-permute-start(bf16[96,896]{1,0:T(8,128)(2,1)S(1)} %get-tuple-element.89), channel_id=1, source_target_pairs={{0,64},{1,65},{2,66},{3,67},{4,68},{5,69},{6,70},{7,71},{8,72},{9,... | collective-permute-start | bytes 516104 | tf_op jit(solution)/shard_map/ppermute | solution.py:42
  102.2 8.4 %collective-permute-start.19 = (bf16[96,896]{1,0:T(8,128)(2,1)S(1)}, bf16[96,896]{1,0:T(8,128)(2,1)S(1)}, u32[]{:S(2)}, u32[]{:S(2)}) collective-permute-start(bf16[96,896]{1,0:T(8,128)(2,1)S(1)} %get-tuple-element.90), channel_id=1, source_target_pairs={{0,32},{1,33},{2,34},{3,35},{4,36},{5,37},{6,38},{7,39},{8,40},{9,... | collective-permute-start | bytes 516104 | tf_op jit(solution)/shard_map/ppermute | solution.py:42
  103.0 8.5 %collective-permute-start.20 = (bf16[96,896]{1,0:T(8,128)(2,1)S(1)}, bf16[96,896]{1,0:T(8,128)(2,1)S(1)}, u32[]{:S(2)}, u32[]{:S(2)}) collective-permute-start(bf16[96,896]{1,0:T(8,128)(2,1)S(1)} %get-tuple-element.91), channel_id=1, source_target_pairs={{0,96},{1,97},{2,98},{3,99},{4,100},{5,101},{6,102},{7,103},{8,104... | collective-permute-start | bytes 516104 | tf_op jit(solution)/shard_map/ppermute | solution.py:42
